TPU v7x, 128 devices: a whole 4x4x4 slice. The times are simulated.
128 devices in a mesh: mp: 16 (over z, y_hi, core), dp: 8 (over y_lo, x).
Axes of the slice: x: 4, y: 4 (y_hi: 2, y_lo: 2; y = y_hi * 2 + y_lo), z: 4, core: 2. Of those that a mesh axis runs over, the one named last changes fastest.
Arguments:
- inputs: bfloat16 [16384, 512], P('dp', 'mp'), may hold values from -45 to 45
- out_grad: bfloat16 [16384, 512], P('dp', 'mp'), may hold values from -6 to 6
- shape_pick: int32 [8], P('dp'), may hold values from 0 to 1, as said below
- filters: bfloat16 [24, 2048], replicated, may hold values from -0.125 to 0.125
- stu_gain: bfloat16 [512], P('mp'), may hold values from 0.25 to 1.75
- stu_weight: bfloat16 [27, 512, 512], P(None, 'mp'), may hold values from -0.0546875 to 0.0546875
- mlp_gain_a: bfloat16 [512], P('mp'), may hold values from 0.25 to 1.75
- gate_a: bfloat16 [512, 2048], P(None, 'mp'), may hold values from -0.25 to 0.25
- up_a: bfloat16 [512, 2048], P(None, 'mp'), may hold values from -0.25 to 0.25
- down_a: bfloat16 [2048, 512], P('mp'), may hold values from -0.125 to 0.125
- attn_gain: bfloat16 [512], P('mp'), may hold values from 0.25 to 1.75
- qkv_weight: bfloat16 [512, 1536], P(None, 'mp'), may hold values from -0.25 to 0.25
- out_weight: bfloat16 [512, 512], P('mp'), may hold values from -3 to 3
- mlp_gain_b: bfloat16 [512], P('mp'), may hold values from 0.25 to 1.75
- gate_b: bfloat16 [512, 2048], P(None, 'mp'), may hold values from -0.25 to 0.25
- up_b: bfloat16 [512, 2048], P(None, 'mp'), may hold values from -0.25 to 0.25
- down_b: bfloat16 [2048, 512], P('mp'), may hold values from -0.125 to 0.125
Outputs:
- output: bfloat16 [16384, 512], P('dp', 'mp')
- input_grad: float32 [16384, 512], P('dp', 'mp')
- stu_gain_grad: float32 [512], P('mp')
- stu_weight_grad: float32 [27, 512, 512], P(None, 'mp')
- mlp_gain_a_grad: float32 [512], P('mp')
- gate_a_grad: float32 [512, 2048], P(None, 'mp')
- up_a_grad: float32 [512, 2048], P(None, 'mp')
- down_a_grad: float32 [2048, 512], P('mp')
- attn_gain_grad: float32 [512], P('mp')
- qkv_weight_grad: float32 [512, 1536], P(None, 'mp')
- out_weight_grad: float32 [512, 512], P('mp')
- mlp_gain_b_grad: float32 [512], P('mp')
- gate_b_grad: float32 [512, 2048], P(None, 'mp')
- up_b_grad: float32 [512, 2048], P(None, 'mp')
- down_b_grad: float32 [2048, 512], P('mp')
Inputs may be any that keep to these rules, and one draw needn't show every extreme that they name: `shape_pick`: 1 makes the sequence one row of 2048 tokens, 0 two rows of 1024 tokens; both occur in every draw.
All inputs are finite; a program needn't handle non-finite values.
Results may differ from a plain program's by a relative error of at most 0.04.
Values may be sent and summed in bfloat16 or wider, within the bound.
A program may use at most 128 MiB of HBM per device.

v0:
```python
import jax
import jax.numpy as jnp
from jax import lax
from jax.experimental import pallas as pl
from jax.experimental.pallas import tpu as pltpu
from jax.sharding import PartitionSpec as P

D = 512
T = 2048
OWN = 128
CH = 32
K = 24
LAGS = 3
FEAT = (K + LAGS) * CH
HD = 64
MP = 16
DP = 8
CHIPS = 8
EPSILON = 1e-05
NEG = -1e30
F32 = jnp.float32
BF16 = jnp.bfloat16
MESH = pl.DeviceIdType.MESH
VMEM = pl.BlockSpec(memory_space=pltpu.VMEM)
SMEM = pl.BlockSpec(memory_space=pltpu.SMEM)
ANY = pl.BlockSpec(memory_space=pl.ANY)
LIMIT = 62 * 2**20


def nn(left, right):
    return jnp.dot(left, right, preferred_element_type=F32)


def tn(left, right):
    return lax.dot_general(left, right, (((0,), (0,)), ((), ())), preferred_element_type=F32)


def nt(left, right):
    return lax.dot_general(left, right, (((1,), (1,)), ((), ())), preferred_element_type=F32)


class Place:
    def __init__(self):
        self.me = lax.axis_index("mp")
        self.z = self.me // 4
        self.chip = self.me // 2
        self.y = self.chip % 2
        self.core = self.me % 2
        self.dp = lax.axis_index("dp")
        self.x = self.dp % 4
        self.ylo = self.dp // 4
        self.partner = self.me + 1 - 2 * self.core
        self.across = self.me + 2 - 4 * self.y
        self.query_core = ((self.z + 1) // 2) % 2
        self.quarters = (self.core, 3 - self.core)

    def around(self, step):
        return (self.me + step) % MP

    def chip_at(self, step):
        return (self.chip + step) % CHIPS

    def along_z(self, step):
        return ((self.z + step) % 4) * 4 + self.me % 4

    def along_x(self, step):
        return {"dp": self.dp - self.x + (self.x + step) % 4}

    def along_dp(self, step):
        return (self.dp + step) % DP


def half(index):
    return pl.ds(pl.multiple_of(index * OWN, OWN), OWN)


def rows(index, count):
    return pl.ds(pl.multiple_of(index * count, count), count)


def remote(src, dst, sems, slot, target):
    return pltpu.make_async_remote_copy(
        src_ref=src,
        dst_ref=dst,
        send_sem=sems.at[0, slot],
        recv_sem=sems.at[1, slot],
        device_id=target if isinstance(target, dict) else {"mp": target},
        device_id_type=MESH,
    )


def greet(targets):
    barrier = pltpu.get_barrier_semaphore()
    for target in targets:
        where = target if isinstance(target, dict) else {"mp": target}
        pl.semaphore_signal(barrier, inc=1, device_id=where, device_id_type=MESH)
    pl.semaphore_wait(barrier, len(targets))


def sems(count):
    return pltpu.SemaphoreType.DMA((2, count))


def norm_forward(stream, gain):
    scaling = lax.rsqrt(jnp.sum(stream * stream, axis=0, keepdims=True) / D + EPSILON)
    return stream * scaling * gain, scaling


def norm_backward(upstream, stream, gain):
    scaling = lax.rsqrt(jnp.sum(stream * stream, axis=0, keepdims=True) / D + EPSILON)
    gain_grad = jnp.sum(upstream * stream * scaling, axis=1, keepdims=True)
    scaled = upstream * gain
    inner = jnp.sum(scaled * stream, axis=0, keepdims=True)
    return scaled * scaling - stream * (scaling * scaling * scaling * inner / D), gain_grad


def swap(place, src, dst, sem, slot=0):
    copy = remote(src, dst, sem, slot, place.across)
    copy.start()
    return copy


def share(place, src, dst, sem, slot):
    copy = remote(src, dst, sem, slot, place.partner)
    copy.start()
    return copy


def hidden_weights(ref):
    return [ref[:, :, group * OWN : (group + 1) * OWN].reshape(2 * D, D) for group in range(3)]


def hidden_backward(weights, normed, grad, acts, where):
    w_gate, w_up, w_down = weights
    gate = nn(w_gate, normed)
    up = nn(w_up, normed)
    sig = jax.nn.sigmoid(gate)
    hidden_grad = nn(w_down, grad)
    gate_grad = (hidden_grad * up * sig * (1.0 + gate * (1.0 - sig))).astype(BF16)
    up_grad = (hidden_grad * gate * sig).astype(BF16)
    acts[0, :, where] = gate_grad
    acts[1, :, where] = up_grad
    acts[2, :, where] = (gate * sig * up).astype(BF16)
    return tn(w_gate, gate_grad) + tn(w_up, up_grad)


def hidden_weight_grads(acts, acts_got, inputs, out):
    for group, (right, right_got) in enumerate(inputs):
        value = (nt(acts[group, :D], right[...]) + nt(acts_got[group], right_got[...])).astype(BF16)
        for index in range(4):
            out[index, group * OWN : (group + 1) * OWN] = value[index * OWN : (index + 1) * OWN]


def gather_all(place, buf, sem):
    own = buf.at[:, half(place.me)]
    sends = [
        remote(own, own, sem, step - 1, place.chip_at(step) * 2 + place.core) for step in range(1, CHIPS)
    ]
    forwards = [remote(own, own, sem, 7, place.partner)]
    for step in range(1, CHIPS):
        here = buf.at[:, half(place.chip_at(CHIPS - step) * 2 + place.core)]
        forwards.append(remote(here, here, sem, 7 + step, place.partner))

    def spread_own():
        for copy in sends + forwards[:1]:
            copy.start()

    def forward():
        for step in range(1, CHIPS):
            sends[step - 1].wait_recv()
            forwards[step].start()

    def close():
        for copy in sends:
            copy.wait_send()
        for copy in forwards:
            copy.wait()

    return spread_own, forward, close


def toeplitz(taps):
    wide = pltpu.roll(jnp.broadcast_to(taps, (OWN, T)), 0, 1, stride=1, stride_axis=0)
    lane = lax.broadcasted_iota(jnp.int32, (OWN, OWN), 1)
    row = lax.broadcasted_iota(jnp.int32, (OWN, OWN), 0)
    first = jnp.where(lane >= row, wide[:, :OWN], 0.0)
    return jnp.concatenate([first.astype(BF16), wide[:, OWN:].astype(BF16)], axis=1)


def reverse_taps(taps_ref, reverse):
    row = lax.broadcasted_iota(jnp.int32, (2 * OWN, OWN), 0)
    lane = lax.broadcasted_iota(jnp.int32, (2 * OWN, OWN), 1)
    inside = (lane >= 1) & (row == OWN - lane)
    edge = (lane == 0) & (row == OWN)
    flip = jnp.where(inside | edge, 1.0, 0.0).astype(BF16)
    for index in range(T // OWN):
        begin = T - (index + 1) * OWN
        piece = taps_ref[:, begin : begin + min(2 * OWN, T - begin)]
        reverse[:, index * OWN : (index + 1) * OWN] = nn(piece, flip[: piece.shape[1]])
    reverse[:, T : T + OWN] = nn(taps_ref[:, :OWN], flip[OWN:])
    reverse[:, T + OWN :] = jnp.zeros((K, OWN), F32)


def toeplitz_down(reverse, store):
    wide = pltpu.roll(jnp.broadcast_to(reverse, (OWN, T + 2 * OWN)), 0, 1, stride=1, stride_axis=0).astype(BF16)
    for block in range(T // OWN):
        begin = T - block * OWN
        store(block, wide[:, begin : begin + 2 * OWN])


def lag_mask(shift, pick):
    lane = lax.broadcasted_iota(jnp.int32, (CH, T), 1)
    inner = lane % (T // 2)
    return (lane >= shift) & ((inner >= shift) | (pick == 1))


def spread(qkv_ref, keys, values):
    for index in range(MP):
        keys[:, index * OWN : (index + 1) * OWN] = qkv_ref[index, HD : 2 * HD]
        values[:, index * OWN : (index + 1) * OWN] = qkv_ref[index, 2 * HD :]


def query_block(qkv_ref, quarter):
    parts = [qkv_ref[quarter * 4 + index, :HD] for index in range(4)]
    return jnp.concatenate(parts, axis=1) * jnp.asarray(HD**-0.5, BF16)


def score_mask(quarter, chunk, pick):
    query = quarter * 512 + lax.broadcasted_iota(jnp.int32, (512, 512), 1)
    key = chunk * 512 + lax.broadcasted_iota(jnp.int32, (512, 512), 0)
    same_half = (quarter // 2) == (chunk // 2)
    return (key <= query) & (same_half | (pick == 1))


class GradientSum:
    def __init__(self, place, parts, done, bufs, sem):
        self.place, self.parts, self.done, self.sem = place, parts, done, sem
        self.x_got, self.x_sum, self.y_got, self.y_sum, self.z_got = bufs
        self.copies = []

    def over_x(self):
        place = self.place
        for step in range(1, 4):
            there = (place.x + step) % 4
            copy = remote(
                self.parts.at[:, rows(there, 96)], self.x_got.at[step - 1], self.sem, step - 1, place.along_x(step)
            )
            copy.start()
            self.copies.append(copy)

    def over_y(self):
        place = self.place
        for copy in self.copies[:3]:
            copy.wait_recv()
        value = self.parts[:, rows(place.x, 96)].astype(F32)
        for index in range(3):
            value = value + self.x_got[index].astype(F32)
        self.x_sum[...] = value.astype(BF16)
        there = {"dp": place.dp + 4 - 8 * place.ylo}
        copy = remote(self.x_sum.at[:, rows(1 - place.ylo, 48)], self.y_got, self.sem, 3, there)
        copy.start()
        self.copies.append(copy)

    def over_z(self):
        place = self.place
        self.copies[3].wait_recv()
        value = self.x_sum[:, rows(place.ylo, 48)].astype(F32) + self.y_got[...].astype(F32)
        self.y_sum[...] = value.astype(BF16)
        for step in range(1, 4):
            copy = remote(self.y_sum.at[step], self.z_got.at[step - 1], self.sem, 3 + step, place.along_z(step))
            copy.start()
            self.copies.append(copy)

    def back(self):
        place = self.place
        for copy in self.copies[4:7]:
            copy.wait_recv()
        value = self.y_sum[0].astype(F32)
        for index in range(3):
            value = value + self.z_got[index].astype(F32)
        part = place.x * 2 + place.ylo
        self.done[rows(part, 48), :] = value.astype(BF16)
        mine = self.done.at[rows(part, 48)]
        for step in range(1, DP):
            copy = remote(mine, mine, self.sem, 6 + step, {"dp": place.along_dp(step)})
            copy.start()
            self.copies.append(copy)

    def close(self):
        for copy in self.copies[:7]:
            copy.wait_send()
        for copy in self.copies[7:]:
            copy.wait()


def first_kernel(
    pick_ref, x_ref, go_ref, gains_ref, taps_ref, weight_ref,
    gate_a, up_a, down_a, qkv_w, out_w, gate_b, up_b, down_b,
    scale_ref, feat_out, x1_ref, x2_ref, na_out, qkv_out, wa_out, wat_out, gains_all,
    lse_ref, of_ref, go_heads, gx3_ref, out_ref, n3_all, gwo_ref, gmlp_ref, ggain_ref,
    feat_ref, na_ref, qkv_ref, wa_ref, wat_ref, x_own, go2, squares, taps, table, weight_t, blocks, y_ref,
    core_got, chip_got, parts, got, heads, wb_ref, keys, values, own_heads, all_heads, x3_ref, nb, nb_got, go_got,
    acts, acts_got, parts_n, got_n, parts_z, got_z, grad_heads, out_own,
    sem_s, sem_x, sem_go, sem_gain, sem_wa, sem_wb, sem_wat, sem_y, sem_n, sem_g, sem_z, sem_q,
    sem_o, sem_nb, sem_gn, sem_zb, sem_h, sem_out, sem_all, sem_act, sem_save,
):
    place = Place()
    me, chip, core, x = place.me, place.chip, place.core, place.x
    count = T // OWN
    pick = pick_ref[0]
    stream = x_ref[...].astype(F32)
    squares[pl.ds(me, 1)] = jnp.sum(stream * stream, axis=0, keepdims=True)[None]
    for ref, (gate, up, down) in ((wa_ref, (gate_a, up_a, down_a)), (wb_ref, (gate_b, up_b, down_b))):
        ref[0, 0, :OWN] = gate[...].T
        ref[0, 0, OWN : 2 * OWN] = up[...].T
        ref[0, 0, 2 * OWN :] = down[...]
    wat_ref[chip, core, : 3 * CH] = qkv_w[...]
    wat_ref[chip, core, 3 * CH :] = out_w[...]
    greet([place.around(step) for step in range(1, MP)] + [place.along_x(step) for step in range(1, 4)])
    sums, late, fetch_a, fetch_b, fetch_t, rest_a, rest_b, rest_t = [], [], [], [], [], [], [], []
    for step in range(1, MP):
        there = place.around(step)
        copy = remote(squares.at[me], squares.at[me], sem_s, step - 1, there)
        copy.start()
        sums.append(copy)
    for step in range(1, 4):
        copy = remote(
            wa_ref.at[0, 0, rows(x, 96)], wa_ref.at[0, 4 - step, rows(x, 96)], sem_wa, step - 1, place.along_z(step)
        )
        copy.start()
        fetch_a.append(copy)
    mine_t = wat_ref.at[chip, core, rows(x, CH)]
    for step in range(1, CHIPS):
        copy = remote(mine_t, mine_t, sem_wat, step - 1, place.chip_at(step) * 2 + core)
        copy.start()
        fetch_t.append(copy)
    for step in range(1, MP):
        there = place.around(step)
        for src, dst, sem in (
            (x_ref.at[:, half(there)], x_own.at[rows(me, CH)], sem_x),
            (go_ref.at[:, half(there)], go2.at[rows(me, CH), :OWN], sem_go),
            (gains_ref, gains_all.at[rows(me, CH)], sem_gain),
        ):
            copy = remote(src, dst, sem, step - 1, there)
            copy.start()
            late.append(copy)
    for step in range(1, 4):
        copy = remote(
            wb_ref.at[0, 0, rows(x, 96)], wb_ref.at[0, 4 - step, rows(x, 96)], sem_wb, step - 1, place.along_z(step)
        )
        copy.start()
        fetch_b.append(copy)
    share_a = [share(place, wa_ref.at[0, 0], wa_ref.at[1, 0], sem_wa, 6)]
    share_b = [share(place, wb_ref.at[0, 0], wb_ref.at[1, 0], sem_wb, 6)]
    x_own[rows(me, CH), :] = x_ref[:, half(me)]
    go2[rows(me, CH), :OWN] = go_ref[:, half(me)]
    gains_all[rows(me, CH)] = gains_ref[...]
    taps[...] = taps_ref[...].astype(F32)
    weight_t[...] = weight_ref[...].T

    @pl.loop(0, K // 2)
    def _(step):
        for index in range(2):
            filter_table = toeplitz(taps[pl.ds(step * 2 + index, 1), :])
            for offset in range(count):
                table[step, offset * OWN : (offset + 1) * OWN, index * OWN : (index + 1) * OWN] = filter_table[
                    :, offset * OWN : (offset + 1) * OWN
                ]

    for copy in sums:
        copy.wait()
    total = squares[0]
    for index in range(1, MP):
        total = total + squares[index]
    scaling = lax.rsqrt(total / D + EPSILON)
    scale_ref[...] = scaling
    own = stream * scaling * gains_ref[:, 3:4].astype(F32)
    h = own.astype(BF16)
    own = h.astype(F32)
    joined = jnp.full((CH, OWN), (pick == 1).astype(F32)).astype(BF16)
    for target in range(count):
        for offset in range(count):
            here = (slice(target * CH, (target + 1) * CH), slice(offset * OWN, (offset + 1) * OWN))
            if offset > target:
                blocks[here] = jnp.zeros((CH, OWN), BF16)
                continue
            source = target - offset
            value = h[:, source * OWN : (source + 1) * OWN]
            if target >= count // 2 and source < count // 2:
                value = value * joined
            blocks[here] = value
    for shift in range(LAGS):
        moved = own if shift == 0 else pltpu.roll(own, shift, 1)
        moved = jnp.where(lag_mask(shift, pick), moved, 0.0).astype(BF16)
        feat_ref[(K + shift) * CH : (K + shift + 1) * CH, :] = moved

    def convolve(step):
        early = nn(blocks[: CH * count // 2, : T // 2], table[step, : T // 2, :]).astype(BF16)
        late_half = nn(blocks[CH * count // 2 :, :], table[step]).astype(BF16)
        for index in range(2):
            base = pl.multiple_of((step * 2 + index) * CH, CH)
            for target in range(count):
                part, at = (early, target) if target < count // 2 else (late_half, target - count // 2)
                feat_ref[pl.ds(base, CH), target * OWN : (target + 1) * OWN] = part[
                    at * CH : (at + 1) * CH, index * OWN : (index + 1) * OWN
                ]


    def pass_on(fetched, source, sem, done, rest):
        for copy in fetched:
            copy.wait_recv()
        for step in range(1, 4):
            copy = remote(source, source, sem, done + step - 1, place.along_x(step))
            copy.start()
            rest.append(copy)

    pl.loop(0, K // 4)(convolve)
    pass_on(fetch_a, wa_ref.at[0, 1:4, rows(x, 96)], sem_wa, 3, rest_a)
    pl.loop(K // 4, K // 2)(convolve)
    saves = []

    def save(src, dst):
        copy = pltpu.make_async_copy(src, dst, sem_save.at[len(saves)])
        copy.start()
        saves.append(copy)

    save(feat_ref, feat_out)
    for group in range(4):
        y = nn(weight_t[...], feat_ref[:, group * 512 : (group + 1) * 512]).astype(BF16)
        for index in range(4):
            y_ref[group * 2 + index // 2, index % 2] = y[:, index * OWN : (index + 1) * OWN]
    order = list(range(1, CHIPS)) + [0]
    first, second = [], []
    for step in order:
        there = place.chip_at(step)
        copy = remote(y_ref.at[there, 1 - core], core_got.at[there], sem_y, step, place.partner)
        copy.start()
        first.append(copy)
    for copy, step in zip(first, order):
        there = place.chip_at(step)
        copy.wait_recv()
        total = y_ref[there, core].astype(F32) + core_got[there].astype(F32)
        if step == 0:
            x1_ref[...] = total
        else:
            y_ref[there, core] = total.astype(BF16)
            move = remote(y_ref.at[there, core], chip_got.at[step - 1], sem_y, 7 + step, there * 2 + core)
            move.start()
            second.append(move)
    pass_on(fetch_t, wat_ref.at[:, core, rows(x, CH)], sem_wat, 7, rest_t)
    for copy in late:
        copy.wait()
    move_go = swap(place, go2.at[:, :OWN], go2.at[:, OWN:], sem_g)
    for copy in rest_a:
        copy.wait_recv()
    share_a.append(share(place, wa_ref.at[0, 1:], wa_ref.at[1, 1:], sem_wa, 7))
    for move in second:
        move.wait_recv()
    x1 = x1_ref[...] + x_own[...].astype(F32)
    for index in range(CHIPS - 1):
        x1 = x1 + chip_got[index].astype(F32)
    x1_ref[...] = x1
    normed, _ = norm_forward(x1, gains_all[:, 0:1].astype(F32))
    na_ref[:, :OWN] = normed.astype(BF16)
    move_n = swap(place, na_ref.at[:, :OWN], na_ref.at[:, OWN:], sem_n)
    for copy in share_a:
        copy.wait_recv()
    save(wa_ref, wa_out)
    w_gate, w_up, w_down = hidden_weights(wa_ref)

    def forward(normed):
        gate = nn(w_gate, normed)
        hidden = (gate * jax.nn.sigmoid(gate) * nn(w_up, normed)).astype(BF16)
        return tn(w_down, hidden)

    z = forward(na_ref[:, :OWN])
    pass_on(fetch_b, wb_ref.at[0, 1:4, rows(x, 96)], sem_wb, 3, rest_b)
    move_n.wait_recv()
    parts[...] = forward(na_ref[:, OWN:]).astype(BF16)
    move_z = swap(place, parts, got, sem_z)
    save(na_ref, na_out)
    for copy in rest_t:
        copy.wait_recv()
    half_t = wat_ref.at[:, core]
    share_t = share(place, half_t, half_t, sem_wat, 10)
    move_z.wait_recv()
    x2 = x1 + z + got[...].astype(F32)
    x2_ref[...] = x2
    n3 = norm_forward(x2, gains_all[:, 1:2].astype(F32))[0].astype(BF16)
    n3_all[:, half(me)] = n3
    share_t.wait_recv()
    save(wat_ref, wat_out)
    w_qkv = wat_ref[:, :, : 3 * CH].reshape(3 * D, D)
    heads[...] = nn(w_qkv, n3).astype(BF16).reshape(CHIPS, 3 * HD, OWN)
    sends = []
    for step in range(1, CHIPS):
        there = place.chip_at(step)
        copy = remote(heads.at[there], qkv_ref.at[me], sem_q, step - 1, there * 2 + core)
        copy.start()
        sends.append(copy)
    qkv_ref[me] = heads[chip]
    forwards = [remote(qkv_ref.at[me], qkv_ref.at[me], sem_q, 7, place.partner)]
    forwards[0].start()
    for step in range(1, CHIPS):
        source = place.chip_at(CHIPS - step) * 2 + core
        sends[step - 1].wait_recv()
        copy = remote(qkv_ref.at[source], qkv_ref.at[source], sem_q, 7 + step, place.partner)
        copy.start()
        forwards.append(copy)
    for copy in forwards:
        copy.wait()
    save(qkv_ref, qkv_out)
    for copy in rest_b:
        copy.wait_recv()
    share_b.append(share(place, wb_ref.at[0, 1:], wb_ref.at[1, 1:], sem_wb, 7))
    for copy in fetch_a + fetch_b + fetch_t + rest_a + rest_t + share_a + [share_t] + first + second + sends:
        copy.wait_send()
    move_go.wait()
    move_n.wait_send()
    move_z.wait_send()
    spread_n3, forward_n3, close_n3 = gather_all(place, n3_all, sem_all)
    spread_n3()
    spread(qkv_ref, keys, values)
    for part in range(2):
        quarter = place.quarters[part]
        queries = query_block(qkv_ref, quarter)
        top = jnp.full((1, 512), NEG, F32)
        norm = jnp.zeros((1, 512), F32)
        total = jnp.zeros((HD, 512), F32)
        for chunk in range(2 + 2 * part):
            here = slice(chunk * 512, (chunk + 1) * 512)
            scores = jnp.where(score_mask(quarter, chunk, pick), tn(keys[:, here], queries), NEG)
            new_top = jnp.maximum(top, jnp.max(scores, axis=0, keepdims=True))
            weights = jnp.exp(scores - new_top)
            rescale = jnp.exp(top - new_top)
            norm = norm * rescale + jnp.sum(weights, axis=0, keepdims=True)
            total = total * rescale + nn(values[:, here], weights.astype(BF16))
            top = new_top
        total = total / norm
        lse_ref[part] = top + jnp.log(norm)
        of_ref[part] = total
        for index in range(4):
            own_heads[part * 4 + index] = total[:, index * OWN : (index + 1) * OWN].astype(BF16)
    targets = [place.quarters[slot // 4] * 4 + slot % 4 for slot in range(8)]
    copies = [
        pltpu.make_async_remote_copy(
            src_ref=own_heads.at[slot], dst_ref=all_heads.at[chip],
            send_sem=sem_o.at[0, slot], recv_sem=sem_o.at[1, chip],
            device_id={"mp": targets[slot]}, device_id_type=MESH,
        )
        for slot in range(8)
    ]
    for slot in range(8):
        pl.when(targets[slot] != me)(copies[slot].start)

        @pl.when(targets[slot] == me)
        def _():
            all_heads[chip] = own_heads[slot]

    arrivals = [
        remote(own_heads.at[0], all_heads.at[head], sem_o, head, place.partner) for head in range(CHIPS)
    ]
    for head in range(CHIPS):
        pl.when(head * 2 + place.query_core != me)(arrivals[head].wait_recv)
    w_out = wat_ref[:, :, 3 * CH :].reshape(D, D)
    outputs = all_heads[...].reshape(D, OWN)
    x3 = x2 + tn(w_out, outputs)
    x3_ref[...] = x3
    gain_b = gains_all[:, 2:3].astype(F32)
    nb[:, :OWN] = norm_forward(x3, gain_b)[0].astype(BF16)
    move_n = swap(place, nb.at[:, :OWN], nb.at[:, OWN:], sem_nb)
    for copy in share_b:
        copy.wait_recv()
    weights = hidden_weights(wb_ref)
    normed_grad = hidden_backward(weights, nb[:, :OWN], go2[:, :OWN], acts, slice(0, OWN))
    move_n.wait_recv()
    parts_n[...] = hidden_backward(
        weights, nb[:, OWN:], go2[:, OWN:], acts, slice(OWN, 2 * OWN)
    ).astype(BF16)
    move_gn = swap(place, parts_n, got_n, sem_gn)
    shares = [
        share(place, acts.at[:, D:], acts_got, sem_act, 0),
        share(place, nb, nb_got, sem_act, 1),
        share(place, go2, go_got, sem_act, 2),
    ]
    parts_z[...] = tn(weights[2], acts[2, :, OWN:]).astype(BF16)
    move_z = swap(place, parts_z, got_z, sem_zb)
    z = tn(weights[2], acts[2, :, :OWN])
    move_gn.wait_recv()
    normed_grad = normed_grad + got_n[...].astype(F32)
    stream_grad, gain_grad = norm_backward(normed_grad, x3_ref[...], gain_b)
    ggain_ref[...] = gain_grad
    gx3 = go2[:, :OWN].astype(F32) + stream_grad
    gx3_ref[...] = gx3
    gy = gx3.astype(BF16)
    grad_heads[...] = nn(w_out, gy).astype(BF16).reshape(CHIPS, HD, OWN)
    slot = (place.z // 2) * 4 + me % 4
    sends = [
        pltpu.make_async_remote_copy(
            src_ref=grad_heads.at[head], dst_ref=go_heads.at[slot],
            send_sem=sem_h.at[0, head], recv_sem=sem_h.at[1, slot],
            device_id={"mp": head * 2 + place.query_core}, device_id_type=MESH,
        )
        for head in range(CHIPS)
    ]
    for head in range(CHIPS):
        pl.when(head * 2 + place.query_core != me)(sends[head].start)

        @pl.when(head * 2 + place.query_core == me)
        def _():
            go_heads[slot] = grad_heads[head]

    move_z.wait_recv()
    out_own[...] = (x3_ref[...] + z + got_z[...].astype(F32)).astype(BF16)
    moves = []
    for step in range(1, MP):
        there = place.around(step)
        copy = remote(out_own.at[rows(there, CH)], out_ref.at[:, half(me)], sem_out, step - 1, there)
        copy.start()
        moves.append(copy)
    out_ref[:, half(me)] = out_own[rows(me, CH), :]
    forward_n3()
    gwo_ref[...] = nt(outputs, gy).astype(BF16).reshape(MP, CH, D)
    for copy in shares:
        copy.wait_recv()
    hidden_weight_grads(acts, acts_got, ((nb, nb_got), (nb, nb_got), (go2, go_got)), gmlp_ref)
    for slot_in in range(8):
        arrival = remote(grad_heads.at[0], go_heads.at[slot_in], sem_h, slot_in, place.partner)
        pl.when(targets[slot_in] != me)(arrival.wait_recv)
    for slot_out in range(8):
        pl.when(targets[slot_out] != me)(copies[slot_out].wait_send)
        pl.when(slot_out * 2 + place.query_core != me)(sends[slot_out].wait_send)
    for copy in moves:
        copy.wait()
    close_n3()
    for copy in rest_b + share_b + shares + [move_n, move_gn, move_z]:
        copy.wait_send()
    for copy in saves:
        copy.wait()


def first(*operands):
    return pl.pallas_call(
        first_kernel,
        out_shape=(
            jax.ShapeDtypeStruct((1, T), F32),
            jax.ShapeDtypeStruct((FEAT, T), BF16),
            jax.ShapeDtypeStruct((D, OWN), F32),
            jax.ShapeDtypeStruct((D, OWN), F32),
            jax.ShapeDtypeStruct((D, 2 * OWN), BF16),
            jax.ShapeDtypeStruct((MP, 3 * HD, OWN), BF16),
            jax.ShapeDtypeStruct((2, 4, 3 * OWN, D), BF16),
            jax.ShapeDtypeStruct((CHIPS, 2, OWN, D), BF16),
            jax.ShapeDtypeStruct((D, OWN), BF16),
            jax.ShapeDtypeStruct((2, 1, 512), F32),
            jax.ShapeDtypeStruct((2, HD, 512), F32),
            jax.ShapeDtypeStruct((8, HD, OWN), BF16),
            jax.ShapeDtypeStruct((D, OWN), F32),
            jax.ShapeDtypeStruct((CH, T), BF16),
            jax.ShapeDtypeStruct((D, T), BF16),
            jax.ShapeDtypeStruct((MP, CH, D), BF16),
            jax.ShapeDtypeStruct((4, 3 * OWN, D), BF16),
            jax.ShapeDtypeStruct((D, 1), F32),
        ),
        in_specs=[SMEM] + [VMEM] * 13,
        out_specs=(VMEM, ANY, VMEM, VMEM, ANY, ANY, ANY, ANY) + (VMEM,) * 10,
        scratch_shapes=[
            pltpu.VMEM((FEAT, T), BF16),
            pltpu.VMEM((D, 2 * OWN), BF16),
            pltpu.VMEM((MP, 3 * HD, OWN), BF16),
            pltpu.VMEM((2, 4, 3 * OWN, D), BF16),
            pltpu.VMEM((CHIPS, 2, OWN, D), BF16),
            pltpu.VMEM((D, OWN), BF16),
            pltpu.VMEM((D, 2 * OWN), BF16),
            pltpu.VMEM((MP, 1, T), F32),
            pltpu.VMEM((K, T), F32),
            pltpu.VMEM((K // 2, T, 2 * OWN), BF16),
            pltpu.VMEM((D, FEAT), BF16),
            pltpu.VMEM((CH * T // OWN, T), BF16),
            pltpu.VMEM((CHIPS, 2, D, OWN), BF16),
            pltpu.VMEM((CHIPS, D, OWN), BF16),
            pltpu.VMEM((CHIPS - 1, D, OWN), BF16),
            pltpu.VMEM((D, OWN), BF16),
            pltpu.VMEM((D, OWN), BF16),
            pltpu.VMEM((CHIPS, 3 * HD, OWN), BF16),
            pltpu.VMEM((2, 4, 3 * OWN, D), BF16),
            pltpu.VMEM((HD, T), BF16),
            pltpu.VMEM((HD, T), BF16),
            pltpu.VMEM((8, HD, OWN), BF16),
            pltpu.VMEM((8, HD, OWN), BF16),
            pltpu.VMEM((D, OWN), F32),
            pltpu.VMEM((D, 2 * OWN), BF16),
            pltpu.VMEM((D, 2 * OWN), BF16),
            pltpu.VMEM((D, 2 * OWN), BF16),
            pltpu.VMEM((3, 2 * D, 2 * OWN), BF16),
            pltpu.VMEM((3, D, 2 * OWN), BF16),
            pltpu.VMEM((D, OWN), BF16),
            pltpu.VMEM((D, OWN), BF16),
            pltpu.VMEM((D, OWN), BF16),
            pltpu.VMEM((D, OWN), BF16),
            pltpu.VMEM((CHIPS, HD, OWN), BF16),
            pltpu.VMEM((D, OWN), BF16),
            sems(15), sems(15), sems(15), sems(15), sems(8), sems(8), sems(11),
            sems(15), sems(1), sems(1), sems(1), sems(15),
            sems(8), sems(1), sems(1), sems(1), sems(8), sems(15), sems(15), sems(3),
            pltpu.SemaphoreType.DMA((5,)),
        ],
        compiler_params=pltpu.CompilerParams(
            collective_id=0, has_side_effects=True, vmem_limit_bytes=LIMIT
        ),
        name="first",
    )(*operands)


def second_kernel(
    pick_ref, x_ref, scale_ref, feat_in, x1_ref, x2_ref, na_ref, qkv_ref, wa_in, wat_in, gains_all,
    lse_ref, of_ref, go_heads, gx3_ref, n3_in, gwo_ref, gmlp_b, ggain_b, gains_ref, taps_ref, weight_in,
    gx_ref, joint_ref, sum_a, sum_b, gain_sum,
    feat_ref, wa_ref, wat_ref, n3_all, weight_ref,
    keys, values, kv_grad, q_grad, mine, core_got, chip_sum, head_grads, gz, gz_got, na_got, parts, got,
    acts, acts_got, gy1_ref, row_got, q_rows, gwo_got,
    bx_got, bx_sum, by_got, by_sum, bz_got, gmlp_a, ax_got, ax_sum, ay_got, ay_sum, az_got, ggain_ref, gain_got, gain_own, gain_dp,
    reverse, table, feature_grad, shifted, total, gh_ref, joint, joint_got, inner,
    sem_q, sem_n, sem_z, sem_y, sem_gwo, sem_rows, sem_b, sem_a, sem_g, sem_gd, sem_j, sem_jg, sem_p, sem_act, sem_load,
):
    place = Place()
    me, dp, chip, core = place.me, place.dp, place.chip, place.core
    wide = 2 * OWN
    count = T // wide
    loads = []
    for src, dst in (
        (wat_in, wat_ref), (wa_in, wa_ref), (n3_in, n3_all), (feat_in, feat_ref), (weight_in, weight_ref)
    ):
        copy = pltpu.make_async_copy(src, dst, sem_load.at[len(loads)])
        copy.start()
        loads.append(copy)
    greet(
        [place.around(step) for step in range(1, MP)]
        + [{"dp": place.along_dp(step)} for step in range(1, DP)]
    )
    gain_a = gains_all[:, 0:1].astype(F32)
    gain_n = gains_all[:, 1:2].astype(F32)
    sum_of_b = GradientSum(place, gmlp_b, sum_b, (bx_got, bx_sum, by_got, by_sum, bz_got), sem_b)
    sum_of_a = GradientSum(place, gmlp_a, sum_a, (ax_got, ax_sum, ay_got, ay_sum, az_got), sem_a)
    share_n = share(place, na_ref, na_got, sem_act, 0)
    sum_of_b.over_x()
    o_first = []
    for step in range(1, MP):
        there = place.around(step)
        copy = remote(gwo_ref.at[there], gwo_got.at[step - 1], sem_gwo, step - 1, there)
        copy.start()
        o_first.append(copy)
    pick = pick_ref[0]
    spread(qkv_ref, keys, values)
    for part in range(2):
        quarter = place.quarters[part]
        queries = query_block(qkv_ref, quarter)
        out_grad = jnp.concatenate([go_heads[part * 4 + index] for index in range(4)], axis=1)
        weighted = jnp.sum(of_ref[part] * out_grad.astype(F32), axis=0, keepdims=True)
        queries_t = queries.T
        out_grad_t = out_grad.T
        query_grad = jnp.zeros((HD, 512), F32)
        for chunk in range(2 + 2 * part):
            here = slice(chunk * 512, (chunk + 1) * 512)
            scores = tn(keys[:, here], queries) - lse_ref[part]
            probs = jnp.where(score_mask(quarter, chunk, pick), jnp.exp(scores), 0.0)
            score_grad = (probs * (tn(values[:, here], out_grad) - weighted)).astype(BF16)
            query_grad = query_grad + nn(keys[:, here], score_grad)
            key_part = nn(score_grad, queries_t)
            value_part = nn(probs.astype(BF16), out_grad_t)
            both = jnp.concatenate([key_part, value_part], axis=1)
            if part == 1 and chunk < 2:
                both = both + kv_grad[here]
            kv_grad[here] = both
        q_grad[part] = (query_grad * HD**-0.5).astype(BF16)
    for index in range(MP):
        mine[index // 2, index % 2, :HD] = jnp.zeros((HD, OWN), BF16)
        mine[index // 2, index % 2, HD:] = kv_grad[index * OWN : (index + 1) * OWN].T.astype(BF16)
    for part in range(2):
        quarter = place.quarters[part]
        for index in range(4):
            mine[quarter * 2 + index // 2, index % 2, :HD] = q_grad[part, :, index * OWN : (index + 1) * OWN]
    order = list(range(1, CHIPS)) + [0]
    first = []
    for step in order:
        there = place.chip_at(step)
        copy = remote(mine.at[there, 1 - core], core_got.at[there], sem_q, step, place.partner)
        copy.start()
        first.append(copy)
    second = []
    for copy, step in zip(first, order):
        there = place.chip_at(step)
        copy.wait_recv()
        amount = (mine[there, core].astype(F32) + core_got[there].astype(F32)).astype(BF16)
        chip_sum[there] = amount
        if step == 0:
            head_grads[chip] = amount
        else:
            move = remote(chip_sum.at[there], head_grads.at[chip], sem_q, 7 + step, there * 2 + core)
            move.start()
            second.append(move)
    share_q = share(place, chip_sum.at[:, rows(1 - core, 96)], row_got, sem_rows, 0)
    for move in second:
        move.wait_recv()
    loads[0].wait()
    w_qkv = wat_ref[:, :, : 3 * CH].reshape(3 * D, D)
    columns = head_grads[...].reshape(3 * D, OWN)
    stream_grad, gain_grad = norm_backward(tn(w_qkv, columns), x2_ref[...], gain_n)
    lane = lax.broadcasted_iota(jnp.int32, (D, OWN), 1)
    gain_grads = jnp.where(lane == 1, gain_grad, 0.0) + jnp.where(lane == 2, ggain_b[...], 0.0)
    gx2 = gx3_ref[...] + stream_grad
    gz[:, :OWN] = gx2.astype(BF16)
    move_gz = swap(place, gz.at[:, :OWN], gz.at[:, OWN:], sem_n)
    sum_of_b.over_y()
    loads[1].wait()
    weights = hidden_weights(wa_ref)
    normed_grad = hidden_backward(weights, na_ref[:, :OWN], gz[:, :OWN], acts, slice(0, OWN))
    move_gz.wait_recv()
    parts[...] = hidden_backward(
        weights, na_ref[:, OWN:], gz[:, OWN:], acts, slice(OWN, 2 * OWN)
    ).astype(BF16)
    move_gn = swap(place, parts, got, sem_z)
    shares = [
        share_n,
        share(place, acts.at[:, D:], acts_got, sem_act, 1),
        share(place, gz, gz_got, sem_act, 2),
    ]
    sum_of_b.over_z()
    for copy in shares:
        copy.wait_recv()
    hidden_weight_grads(acts, acts_got, ((na_ref, na_got), (na_ref, na_got), (gz, gz_got)), gmlp_a)
    sum_of_a.over_x()
    move_gn.wait_recv()
    normed_grad = normed_grad + got[...].astype(F32)
    stream_grad, gain_grad = norm_backward(normed_grad, x1_ref[...], gain_a)
    ggain_ref[...] = gain_grads + jnp.where(lane == 0, gain_grad, 0.0)
    gy1_ref[:, half(me)] = (gx2 + stream_grad).astype(BF16)
    spread_gy1, forward_gy1, close_gy1 = gather_all(place, gy1_ref, sem_y)
    spread_gy1()
    sum_of_b.back()
    share_q.wait_recv()
    loads[2].wait()
    for index in range(CHIPS):
        q_rows[:, half(index * 2 + core)] = chip_sum[index, rows(core, 96), :]
        q_rows[:, half(index * 2 + 1 - core)] = row_got[index]
    joint[FEAT : FEAT + 3 * CH] = nt(q_rows[...], n3_all[...]).astype(BF16)
    for copy in o_first:
        copy.wait_recv()
    value = gwo_ref[me].astype(F32)
    for index in range(MP - 1):
        value = value + gwo_got[index].astype(F32)
    joint[FEAT + 3 * CH : FEAT + OWN] = value.astype(BF16)
    joint[FEAT + OWN :] = jnp.zeros((CH, D), BF16)
    reverse_taps(taps_ref, reverse)

    def build(filter_index, slot):
        def store(block, value):
            table[slot, block * OWN : (block + 1) * OWN, :] = value

        toeplitz_down(reverse[pl.ds(filter_index, 1), :], store)

    @pl.loop(0, K // 2)
    def _(index):
        build(index, index)

    forward_gy1()
    close_gy1()
    gain_first = []
    for step in range(1, MP):
        there = place.around(step)
        copy = remote(ggain_ref.at[rows(there, CH)], gain_got.at[step - 1], sem_g, step - 1, there)
        copy.start()
        gain_first.append(copy)
    loads[3].wait()
    loads[4].wait()
    joint[:FEAT] = nt(feat_ref[...], gy1_ref[...]).astype(BF16)
    j_first = []
    for step in range(1, DP):
        there = place.along_dp(step)
        copy = remote(joint.at[rows(there, OWN)], joint_got.at[step - 1], sem_j, step - 1, {"dp": there})
        copy.start()
        j_first.append(copy)
    for group in range(4):
        here = slice(group * 512, (group + 1) * 512)
        feature_grad[:, here] = nn(weight_ref[: K * CH], gy1_ref[:, here]).astype(BF16)
    total[...] = jnp.zeros_like(total)
    shifted[...] = jnp.zeros_like(shifted)
    joined = jnp.full((CH, T // 2), (pick == 1).astype(F32)).astype(BF16)
    middle = CH * count // 2

    def convolve(filter_index, slot):
        mine = feature_grad[pl.ds(pl.multiple_of(filter_index * CH, CH), CH), :]
        for source in range(count):
            here = slice(source * CH, (source + 1) * CH)
            begin = source * wide
            if source < count // 2:
                near_end = T // 2 - begin
                shifted[here, :near_end] = mine[:, begin : T // 2]
                shifted[here, near_end : T - begin] = mine[:, T // 2 :] * joined
            else:
                shifted[here, : T - begin] = mine[:, begin:]
        total[:middle] += nn(shifted[:middle, :], table[slot])
        total[middle:] += nn(shifted[middle:, : T // 2], table[slot, : T // 2, :])

    sum_of_a.over_y()

    @pl.loop(0, K // 2)
    def _(index):
        convolve(index, index)

    sum_of_a.over_z()

    @pl.loop(K // 2, K)
    def _(index):
        build(index, index - K // 2)
        convolve(index, index - K // 2)

    for source in range(count):
        gh_ref[:, source * wide : (source + 1) * wide] = total[source * CH : (source + 1) * CH]
    for shift in range(LAGS):
        begin = (K + shift) * CH
        value = nn(weight_ref[begin : begin + CH], gy1_ref[...])
        value = jnp.where(lag_mask(shift, pick), value, 0.0)
        if shift:
            value = pltpu.roll(value, T - shift, 1)
        gh_ref[...] += value
    stream = x_ref[...].astype(F32)
    scaled = gh_ref[...] * gains_ref[:, 3:4].astype(F32)
    inner[pl.ds(me, 1)] = jnp.sum(scaled * stream, axis=0, keepdims=True)[None]
    sums = []
    for step in range(1, MP):
        copy = remote(inner.at[me], inner.at[me], sem_p, step - 1, place.around(step))
        copy.start()
        sums.append(copy)
    last = []
    scaling = scale_ref[...]
    gain_grad = jnp.sum(gh_ref[...] * stream * scaling, axis=1, keepdims=True)
    for copy in gain_first:
        copy.wait_recv()
    value = ggain_ref[rows(me, CH), :]
    for index in range(MP - 1):
        value = value + gain_got[index]
    lane = lax.broadcasted_iota(jnp.int32, (CH, OWN), 1)
    gain_own[...] = value + jnp.where(lane == 3, gain_grad, 0.0)
    for step in range(1, DP):
        copy = remote(gain_own, gain_dp.at[step - 1], sem_gd, step - 1, {"dp": place.along_dp(step)})
        copy.start()
        last.append(copy)
    for copy in j_first:
        copy.wait_recv()
    value = joint[rows(dp, OWN), :].astype(F32)
    for index in range(DP - 1):
        value = value + joint_got[index].astype(F32)
    joint_ref[rows(dp, OWN), :] = value.astype(BF16)
    done_j = joint_ref.at[rows(dp, OWN)]
    for step in range(1, DP):
        copy = remote(done_j, done_j, sem_jg, step - 1, {"dp": place.along_dp(step)})
        copy.start()
        last.append(copy)
    sum_of_a.back()
    for copy in sums:
        copy.wait()
    value = inner[0]
    for index in range(1, MP):
        value = value + inner[index]
    stream_grad = scaled * scaling - stream * (scaling * scaling * scaling * value / D)
    gx_ref[...] = stream_grad + gy1_ref[rows(me, CH), :].astype(F32)
    for copy in last:
        copy.wait()
    value = gain_own[...]
    for index in range(DP - 1):
        value = value + gain_dp[index]
    gain_sum[...] = value
    for copy in first + second + [share_q] + shares + [move_gz, move_gn] + o_first + j_first + gain_first:
        copy.wait_send()
    sum_of_a.close()
    sum_of_b.close()


def second(*operands):
    return pl.pallas_call(
        second_kernel,
        out_shape=(
            jax.ShapeDtypeStruct((CH, T), F32),
            jax.ShapeDtypeStruct((DP * OWN, D), BF16),
            jax.ShapeDtypeStruct((3 * OWN, D), BF16),
            jax.ShapeDtypeStruct((3 * OWN, D), BF16),
            jax.ShapeDtypeStruct((CH, OWN), F32),
        ),
        in_specs=[SMEM, VMEM, VMEM, ANY, VMEM, VMEM, VMEM, VMEM, ANY, ANY]
        + [VMEM] * 5
        + [ANY]
        + [VMEM] * 5
        + [ANY],
        out_specs=(VMEM,) * 5,
        scratch_shapes=[
            pltpu.VMEM((FEAT, T), BF16),
            pltpu.VMEM((2, 4, 3 * OWN, D), BF16),
            pltpu.VMEM((CHIPS, 2, OWN, D), BF16),
            pltpu.VMEM((D, T), BF16),
            pltpu.VMEM((FEAT, D), BF16),
            pltpu.VMEM((HD, T), BF16),
            pltpu.VMEM((HD, T), BF16),
            pltpu.VMEM((T, 2 * HD), F32),
            pltpu.VMEM((2, HD, 512), BF16),
            pltpu.VMEM((CHIPS, 2, 3 * HD, OWN), BF16),
            pltpu.VMEM((CHIPS, 3 * HD, OWN), BF16),
            pltpu.VMEM((CHIPS, 3 * HD, OWN), BF16),
            pltpu.VMEM((CHIPS, 3 * HD, OWN), BF16),
            pltpu.VMEM((D, 2 * OWN), BF16),
            pltpu.VMEM((D, 2 * OWN), BF16),
            pltpu.VMEM((D, 2 * OWN), BF16),
            pltpu.VMEM((D, OWN), BF16),
            pltpu.VMEM((D, OWN), BF16),
            pltpu.VMEM((3, 2 * D, 2 * OWN), BF16),
            pltpu.VMEM((3, D, 2 * OWN), BF16),
            pltpu.VMEM((D, T), BF16),
            pltpu.VMEM((CHIPS, 96, OWN), BF16),
            pltpu.VMEM((96, T), BF16),
            pltpu.VMEM((MP - 1, CH, D), BF16),
            pltpu.VMEM((3, 4, 96, D), BF16),
            pltpu.VMEM((4, 96, D), BF16),
            pltpu.VMEM((4, 48, D), BF16),
            pltpu.VMEM((4, 48, D), BF16),
            pltpu.VMEM((3, 48, D), BF16),
            pltpu.VMEM((4, 3 * OWN, D), BF16),
            pltpu.VMEM((3, 4, 96, D), BF16),
            pltpu.VMEM((4, 96, D), BF16),
            pltpu.VMEM((4, 48, D), BF16),
            pltpu.VMEM((4, 48, D), BF16),
            pltpu.VMEM((3, 48, D), BF16),
            pltpu.VMEM((D, OWN), F32),
            pltpu.VMEM((MP - 1, CH, OWN), F32),
            pltpu.VMEM((CH, OWN), F32),
            pltpu.VMEM((DP - 1, CH, OWN), F32),
            pltpu.VMEM((K, T + 2 * OWN), F32),
            pltpu.VMEM((K // 2, T, 2 * OWN), BF16),
            pltpu.VMEM((K * CH, T), BF16),
            pltpu.VMEM((CH * T // (2 * OWN), T), BF16),
            pltpu.VMEM((CH * T // (2 * OWN), 2 * OWN), F32),
            pltpu.VMEM((CH, T), F32),
            pltpu.VMEM((DP * OWN, D), BF16),
            pltpu.VMEM((DP - 1, OWN, D), BF16),
            pltpu.VMEM((MP, 1, T), F32),
            sems(15), sems(1), sems(1), sems(15), sems(15), sems(1), sems(14), sems(14), sems(15),
            sems(7), sems(7), sems(7), sems(15), sems(3),
            pltpu.SemaphoreType.DMA((5,)),
        ],
        compiler_params=pltpu.CompilerParams(
            collective_id=1, has_side_effects=True, vmem_limit_bytes=LIMIT
        ),
        name="second",
    )(*operands)


def final_kernel(
    joint_ref, a_ref, b_ref, gain_ref,
    gws, gate_ga, up_ga, down_ga, gqkv, gout, gate_gb, up_gb, down_gb, *gain_grads,
):
    gws[...] = joint_ref[:FEAT].astype(F32)
    gqkv[...] = joint_ref[FEAT : FEAT + 3 * CH].astype(F32)
    gout[...] = joint_ref[FEAT + 3 * CH : FEAT + OWN].astype(F32)
    for ref, (gate, up, down) in ((a_ref, (gate_ga, up_ga, down_ga)), (b_ref, (gate_gb, up_gb, down_gb))):
        gate[...] = ref[:OWN].astype(F32).T
        up[...] = ref[OWN : 2 * OWN].astype(F32).T
        down[...] = ref[2 * OWN :].astype(F32)
    columns = gain_ref[...].T
    for index, grad in enumerate(gain_grads):
        grad[...] = columns[index : index + 1]


def final(*operands):
    mlp = [jax.ShapeDtypeStruct(shape, F32) for shape in ((D, OWN), (D, OWN), (OWN, D))]
    return pl.pallas_call(
        final_kernel,
        out_shape=(
            jax.ShapeDtypeStruct((FEAT, D), F32),
            *mlp,
            jax.ShapeDtypeStruct((3 * CH, D), F32),
            jax.ShapeDtypeStruct((CH, D), F32),
            *mlp,
            *[jax.ShapeDtypeStruct((1, CH), F32)] * 4,
        ),
        in_specs=[VMEM] * 4,
        out_specs=(VMEM,) * 13,
        compiler_params=pltpu.CompilerParams(vmem_limit_bytes=LIMIT),
        name="final",
    )(*operands)


def on_device(
    inputs, out_grad, shape_pick, filters, stu_gain, stu_weight,
    mlp_gain_a, gate_a, up_a, down_a, attn_gain, qkv_weight, out_weight,
    mlp_gain_b, gate_b, up_b, down_b,
):
    gains = jnp.stack([mlp_gain_a, attn_gain, mlp_gain_b, stu_gain], axis=1)
    gains = jnp.pad(gains, ((0, 0), (0, OWN - 4)))
    weight = stu_weight.reshape(FEAT, D)
    x = inputs.T
    (
        scaling, features, x1, x2, na, qkv, wa, wat, gains_all,
        lse, of, go_heads, gx3, out, n3_all, gwo, gmlp_b, ggain_b,
    ) = first(
        shape_pick, x, out_grad.T, gains, filters, weight,
        gate_a, up_a, down_a, qkv_weight.T, out_weight, gate_b, up_b, down_b,
    )
    gx, joint, ga, gb, gain_sum = second(
        shape_pick, x, scaling, features, x1, x2, na, qkv, wa, wat, gains_all,
        lse, of, go_heads, gx3, n3_all, gwo, gmlp_b, ggain_b, gains, filters, weight,
    )
    gws, gate_ga, up_ga, down_ga, gqkv, gout, gate_gb, up_gb, down_gb, *gain_grads = final(joint, ga, gb, gain_sum)
    gain_a, gain_n, gain_b, gain_s = (grad.reshape(CH) for grad in gain_grads)
    return (
        out.T, gx.T, gain_s, gws.reshape(K + LAGS, CH, D), gain_a, gate_ga, up_ga, down_ga,
        gain_n, gqkv.T, gout, gain_b, gate_gb, up_gb, down_gb,
    )


def solution(mesh):
    cols, mid, row = P(None, "mp"), P(None, "mp", None), P("mp", None)
    return jax.shard_map(
        on_device,
        mesh=mesh,
        in_specs=(
            P("dp", "mp"), P("dp", "mp"), P("dp"), P(), P("mp"), mid,
            P("mp"), cols, cols, row, P("mp"), cols, row, P("mp"), cols, cols, row,
        ),
        out_specs=(
            P("dp", "mp"), P("dp", "mp"), P("mp"), mid, P("mp"), cols, cols, row,
            P("mp"), cols, row, P("mp"), cols, cols, row,
        ),
        check_vma=False,
    )
```

profile of v0, /device:TPU:0, one launch (start us, length us, event | category | flops | bytes accessed | tf_op | source)
XLA Modules:
  0.0 221.9 jit_solution(10676575609240205532)
XLA Ops:
  1.3 0.7 pad_maximum_fusion
  2.0 0.1 copy.36
  2.1 0.6 pad.4.gains_ref
  2.7 108.8 %first.1 = (f32[1,2048]{1,0:T(1,128)}, bf16[864,2048]{1,0:T(8,128)(2,1)}, f32[512,128]{1,0:T(8,128)}, f32[512,128]{1,0:T(8,128)}, bf16[512,256]{1,0:T(8,128)(2,1...) custom-call(s32[1]{0:T(128)S(6)} %copy.39.pick_ref, ...), custom_call_target="tpu_custom_call" | custom-call | tf_op jit(solution)/shard_map/first/pallas_call | solution.py:643
  111.5 0.0 copy-start.1
  111.5 105.5 %second.1 = (f32[32,2048]{1,0:T(8,128)}, bf16[1024,512]{1,0:T(8,128)(2,1)}, bf16[384,512]{1,0:T(8,128)(2,1)}, bf16[384,512]{1,0:T(8,128)(2,1)}, f32[32,128]{1,0:T(8,128)}) custom-call(s32[1]{0:T(128)S(6)} %copy.39.pick_ref, bf16[32,2048]{1,0:T(8,128)(2,1)} %bitcast.19, f32[1,2048]{1,0:T(1,128)} %get-tuple-element.52.scale_ref, ...), custom_call_target="tpu_custom_call" | custom-call | tf_op jit(solution)/shard_map/second/pallas_call | solution.py:981
  217.0 0.0 copy-start
  217.1 3.5 %final.1 = (f32[864,512]{1,0:T(8,128)}, f32[512,128]{1,0:T(8,128)}, f32[512,128]{1,0:T(8,128)}, f32[128,512]{1,0:T(8,128)}, f32[96,512]{1,0:T(8,128)}, /*index=5...) custom-call(bf16[1024,512]{1,0:T(8,128)(2,1)} %get-tuple-element.70., ...), custom_call_target="tpu_custom_call" | custom-call | tf_op jit(solution)/shard_map/final/pallas_call | solution.py:1074
  220.5 0.0 copy-done.1
  220.5 0.7 copy.40
  221.2 0.0 copy-done
  221.2 0.7 copy.41
Async XLA Ops:
  111.5 109.0 %copy-start.1 = (bf16[32,2048]{1,0:T(8,128)(2,1)S(1)}, bf16[32,2048]{1,0:T(8,128)(2,1)}, u32[]{:S(2)}) copy-start(bf16[32,2048]{1,0:T(8,128)(2,1)} %get-tuple-element.51) | copy-start | bytes 393220
  217.0 4.1 %copy-start = (f32[32,2048]{1,0:T(8,128)S(1)}, f32[32,2048]{1,0:T(8,128)}, u32[]{:S(2)}) copy-start(f32[32,2048]{1,0:T(8,128)} %get-tuple-element.69) | copy-start | bytes 786436
where the time goes:
time: 223 us; the launch traced here: 222 us
  Pallas kernels  218 us (98%)
    pallas_call x1, Pallas kernels, first(): pl.pallas_call(first_kernel, out_shape=(jax.ShapeDtypeStruct((1, T), F32)...  109 us
    pallas_call x1, Pallas kernels, second(): pl.pallas_call(second_kernel, out_shape=(jax.ShapeDtypeStruct((CH, T), F3...  106 us

commit v1 on v0

--- a/solution.py
+++ b/solution.py
@@ -25,6 +25,7 @@
 SMEM = pl.BlockSpec(memory_space=pltpu.SMEM)
 ANY = pl.BlockSpec(memory_space=pl.ANY)
 LIMIT = 62 * 2**20
+EARLY_TABLES = 4
 
 
 def nn(left, right):
@@ -33,6 +34,10 @@
 
 def tn(left, right):
     return lax.dot_general(left, right, (((0,), (0,)), ((), ())), preferred_element_type=F32)
+
+
+def tn_narrow(weights, right):
+    return tn(right, weights).T
 
 
 def nt(left, right):
@@ -50,7 +55,8 @@
         self.x = self.dp % 4
         self.ylo = self.dp // 4
         self.partner = self.me + 1 - 2 * self.core
-        self.across = self.me + 2 - 4 * self.y
+        self.beside = self.me + 2 - 4 * self.y
+        self.across = self.me + 4 - 8 * (self.z % 2)
         self.query_core = ((self.z + 1) // 2) % 2
         self.quarters = (self.core, 3 - self.core)
 
@@ -59,6 +65,9 @@
 
     def chip_at(self, step):
         return (self.chip + step) % CHIPS
+
+    def same_units(self, slot):
+        return ((self.z + 2 * (slot // 2)) % 4) * 4 + ((self.y + slot % 2) % 2) * 2 + self.core
 
     def along_z(self, step):
         return ((self.z + step) % 4) * 4 + self.me % 4
@@ -94,7 +103,7 @@
     for target in targets:
         where = target if isinstance(target, dict) else {"mp": target}
         pl.semaphore_signal(barrier, inc=1, device_id=where, device_id_type=MESH)
-    pl.semaphore_wait(barrier, len(targets))
+    return lambda: pl.semaphore_wait(barrier, len(targets))
 
 
 def sems(count):
@@ -141,7 +150,7 @@
     acts[0, :, where] = gate_grad
     acts[1, :, where] = up_grad
     acts[2, :, where] = (gate * sig * up).astype(BF16)
-    return tn(w_gate, gate_grad) + tn(w_up, up_grad)
+    return (tn(gate_grad, w_gate) + tn(up_grad, w_up)).T
 
 
 def hidden_weight_grads(acts, acts_got, inputs, out):
@@ -151,32 +160,45 @@
             out[index, group * OWN : (group + 1) * OWN] = value[index * OWN : (index + 1) * OWN]
 
 
-def gather_all(place, buf, sem):
-    own = buf.at[:, half(place.me)]
-    sends = [
-        remote(own, own, sem, step - 1, place.chip_at(step) * 2 + place.core) for step in range(1, CHIPS)
-    ]
-    forwards = [remote(own, own, sem, 7, place.partner)]
-    for step in range(1, CHIPS):
-        here = buf.at[:, half(place.chip_at(CHIPS - step) * 2 + place.core)]
-        forwards.append(remote(here, here, sem, 7 + step, place.partner))
-
-    def spread_own():
-        for copy in sends + forwards[:1]:
+class Gather:
+    steps = (1, 3, 2)
+
+    def __init__(self, place, buf, sem):
+        me = place.me
+        own = buf.at[:, half(me)]
+        beside = buf.at[:, half(place.beside)]
+        self.to_beside = remote(own, own, sem, 0, place.beside)
+        self.to_z = [remote(own, own, sem, step, place.along_z(step)) for step in self.steps]
+        self.relays = [remote(beside, beside, sem, 3 + step, place.along_z(step)) for step in self.steps]
+        self.forwards = [remote(own, own, sem, 7, place.partner), remote(beside, beside, sem, 8, place.partner)]
+        for step in self.steps:
+            for shift, other in ((8, me), (11, place.beside)):
+                index = ((place.z + 4 - step) % 4) * 4 + other % 4
+                here = buf.at[:, half(index)]
+                self.forwards.append(remote(here, here, sem, shift + step, place.partner))
+
+    def begin(self):
+        for copy in [self.to_beside, *self.to_z, self.forwards[0]]:
             copy.start()
 
-    def forward():
-        for step in range(1, CHIPS):
-            sends[step - 1].wait_recv()
-            forwards[step].start()
-
-    def close():
-        for copy in sends:
+    def relay(self):
+        self.to_beside.wait_recv()
+        for copy in [*self.relays, self.forwards[1]]:
+            copy.start()
+
+    def arrive(self, index):
+        self.to_z[index].wait_recv()
+        self.forwards[2 + 2 * index].start()
+        self.relays[index].wait_recv()
+        self.forwards[3 + 2 * index].start()
+
+    def joined(self, index):
+        for copy in self.forwards[2 + 2 * index : 4 + 2 * index]:
+            copy.wait_recv()
+
+    def close(self):
+        for copy in [self.to_beside, *self.to_z, *self.relays, *self.forwards]:
             copy.wait_send()
-        for copy in forwards:
-            copy.wait()
-
-    return spread_own, forward, close
 
 
 def toeplitz(taps):
@@ -233,64 +255,82 @@
 
 
 class GradientSum:
-    def __init__(self, place, parts, done, bufs, sem):
+    def __init__(self, place, parts, done, bufs, sem, begin, each, y_first):
         self.place, self.parts, self.done, self.sem = place, parts, done, sem
-        self.x_got, self.x_sum, self.y_got, self.y_sum, self.z_got = bufs
+        self.got, self.sum_1, self.got_2, self.sum_2, self.z_got = bufs
+        self.begin, self.each, self.y_first = begin, each, y_first
         self.copies = []
-
-    def over_x(self):
-        place = self.place
+        self.to_y = [(1 - place.ylo, {"dp": place.dp + 4 - 8 * place.ylo})]
+        self.to_x = [((place.x + step) % 4, place.along_x(step)) for step in range(1, 4)]
+
+    def at(self, index, count, begin=0):
+        return pl.ds(pl.multiple_of(begin + index * count, 16), count)
+
+    def send(self, src, dst, target):
+        copy = remote(src, dst, self.sem, len(self.copies), target)
+        copy.start()
+        self.copies.append(copy)
+
+    def arrived(self, count):
+        for copy in self.copies[-count:]:
+            copy.wait_recv()
+
+    def first(self):
+        count = self.each * (4 if self.y_first else 2)
+        for slot, (there, target) in enumerate(self.to_y if self.y_first else self.to_x):
+            self.send(self.parts.at[:, self.at(there, count, self.begin)], self.got.at[slot], target)
+
+    def second(self):
+        place, each = self.place, self.each
+        here, peers, count = (place.ylo, 1, each * 4) if self.y_first else (place.x, 3, each * 2)
+        self.arrived(peers)
+        value = self.parts[:, self.at(here, count, self.begin)].astype(F32)
+        for slot in range(peers):
+            value = value + self.got[slot].astype(F32)
+        self.sum_1[...] = value.astype(BF16)
+        for slot, (there, target) in enumerate(self.to_x if self.y_first else self.to_y):
+            self.send(self.sum_1.at[:, self.at(there, each)], self.got_2.at[slot], target)
+
+    def third(self):
+        place, each = self.place, self.each
+        here, peers = (place.x, 3) if self.y_first else (place.ylo, 1)
+        self.arrived(peers)
+        value = self.sum_1[:, self.at(here, each)].astype(F32)
+        for slot in range(peers):
+            value = value + self.got_2[slot].astype(F32)
+        self.sum_2[...] = value.astype(BF16)
         for step in range(1, 4):
-            there = (place.x + step) % 4
-            copy = remote(
-                self.parts.at[:, rows(there, 96)], self.x_got.at[step - 1], self.sem, step - 1, place.along_x(step)
-            )
-            copy.start()
-            self.copies.append(copy)
-
-    def over_y(self):
-        place = self.place
-        for copy in self.copies[:3]:
-            copy.wait_recv()
-        value = self.parts[:, rows(place.x, 96)].astype(F32)
-        for index in range(3):
-            value = value + self.x_got[index].astype(F32)
-        self.x_sum[...] = value.astype(BF16)
-        there = {"dp": place.dp + 4 - 8 * place.ylo}
-        copy = remote(self.x_sum.at[:, rows(1 - place.ylo, 48)], self.y_got, self.sem, 3, there)
-        copy.start()
-        self.copies.append(copy)
-
-    def over_z(self):
-        place = self.place
-        self.copies[3].wait_recv()
-        value = self.x_sum[:, rows(place.ylo, 48)].astype(F32) + self.y_got[...].astype(F32)
-        self.y_sum[...] = value.astype(BF16)
-        for step in range(1, 4):
-            copy = remote(self.y_sum.at[step], self.z_got.at[step - 1], self.sem, 3 + step, place.along_z(step))
-            copy.start()
-            self.copies.append(copy)
+            self.send(self.sum_2.at[step], self.z_got.at[step - 1], place.same_units(step))
 
     def back(self):
-        place = self.place
-        for copy in self.copies[4:7]:
-            copy.wait_recv()
-        value = self.y_sum[0].astype(F32)
-        for index in range(3):
-            value = value + self.z_got[index].astype(F32)
-        part = place.x * 2 + place.ylo
-        self.done[rows(part, 48), :] = value.astype(BF16)
-        mine = self.done.at[rows(part, 48)]
+        place, each = self.place, self.each
+        self.arrived(3)
+        value = self.sum_2[0].astype(F32)
+        for slot in range(3):
+            value = value + self.z_got[slot].astype(F32)
+        index = place.ylo * 4 + place.x if self.y_first else place.x * 2 + place.ylo
+        mine = self.at(index, each, self.begin)
+        self.done[mine, :] = value.astype(BF16)
         for step in range(1, DP):
-            copy = remote(mine, mine, self.sem, 6 + step, {"dp": place.along_dp(step)})
-            copy.start()
-            self.copies.append(copy)
+            self.send(self.done.at[mine], self.done.at[mine], {"dp": place.along_dp(step)})
 
     def close(self):
         for copy in self.copies[:7]:
             copy.wait_send()
         for copy in self.copies[7:]:
             copy.wait()
+
+
+def sum_buffers(each, y_first):
+    first, second = (1, 3) if y_first else (3, 1)
+    wide = each * (4 if y_first else 2)
+    return [
+        pltpu.VMEM((first, 4, wide, D), BF16),
+        pltpu.VMEM((4, wide, D), BF16),
+        pltpu.VMEM((second, 4, each, D), BF16),
+        pltpu.VMEM((4, each, D), BF16),
+        pltpu.VMEM((3, each, D), BF16),
+    ]
 
 
 def first_kernel(
@@ -308,15 +348,29 @@
     me, chip, core, x = place.me, place.chip, place.core, place.x
     count = T // OWN
     pick = pick_ref[0]
+    wat_ref[chip, core, : 3 * CH] = qkv_w[...]
+    wat_ref[chip, core, 3 * CH :] = out_w[...]
+    arrived = greet(
+        [place.around(step) for step in range(1, MP)] + [place.along_x(step) for step in range(1, 4)]
+    )
     stream = x_ref[...].astype(F32)
     squares[pl.ds(me, 1)] = jnp.sum(stream * stream, axis=0, keepdims=True)[None]
     for ref, (gate, up, down) in ((wa_ref, (gate_a, up_a, down_a)), (wb_ref, (gate_b, up_b, down_b))):
         ref[0, 0, :OWN] = gate[...].T
         ref[0, 0, OWN : 2 * OWN] = up[...].T
         ref[0, 0, 2 * OWN :] = down[...]
-    wat_ref[chip, core, : 3 * CH] = qkv_w[...]
-    wat_ref[chip, core, 3 * CH :] = out_w[...]
-    greet([place.around(step) for step in range(1, MP)] + [place.along_x(step) for step in range(1, 4)])
+    taps[...] = taps_ref[...].astype(F32)
+
+    def build(step):
+        for index in range(2):
+            filter_table = toeplitz(taps[pl.ds(step * 2 + index, 1), :])
+            for offset in range(count):
+                table[step, offset * OWN : (offset + 1) * OWN, index * OWN : (index + 1) * OWN] = filter_table[
+                    :, offset * OWN : (offset + 1) * OWN
+                ]
+
+    pl.loop(0, EARLY_TABLES)(build)
+    arrived()
     sums, late, fetch_a, fetch_b, fetch_t, rest_a, rest_b, rest_t = [], [], [], [], [], [], [], []
     for step in range(1, MP):
         there = place.around(step)
@@ -325,7 +379,7 @@
         sums.append(copy)
     for step in range(1, 4):
         copy = remote(
-            wa_ref.at[0, 0, rows(x, 96)], wa_ref.at[0, 4 - step, rows(x, 96)], sem_wa, step - 1, place.along_z(step)
+            wa_ref.at[0, 0, rows(x, 96)], wa_ref.at[0, step, rows(x, 96)], sem_wa, step - 1, place.same_units(step)
         )
         copy.start()
         fetch_a.append(copy)
@@ -346,7 +400,7 @@
             late.append(copy)
     for step in range(1, 4):
         copy = remote(
-            wb_ref.at[0, 0, rows(x, 96)], wb_ref.at[0, 4 - step, rows(x, 96)], sem_wb, step - 1, place.along_z(step)
+            wb_ref.at[0, 0, rows(x, 96)], wb_ref.at[0, step, rows(x, 96)], sem_wb, step - 1, place.same_units(step)
         )
         copy.start()
         fetch_b.append(copy)
@@ -355,18 +409,8 @@
     x_own[rows(me, CH), :] = x_ref[:, half(me)]
     go2[rows(me, CH), :OWN] = go_ref[:, half(me)]
     gains_all[rows(me, CH)] = gains_ref[...]
-    taps[...] = taps_ref[...].astype(F32)
     weight_t[...] = weight_ref[...].T
-
-    @pl.loop(0, K // 2)
-    def _(step):
-        for index in range(2):
-            filter_table = toeplitz(taps[pl.ds(step * 2 + index, 1), :])
-            for offset in range(count):
-                table[step, offset * OWN : (offset + 1) * OWN, index * OWN : (index + 1) * OWN] = filter_table[
-                    :, offset * OWN : (offset + 1) * OWN
-                ]
-
+    pl.loop(EARLY_TABLES, K // 2)(build)
     for copy in sums:
         copy.wait()
     total = squares[0]
@@ -450,7 +494,6 @@
     pass_on(fetch_t, wat_ref.at[:, core, rows(x, CH)], sem_wat, 7, rest_t)
     for copy in late:
         copy.wait()
-    move_go = swap(place, go2.at[:, :OWN], go2.at[:, OWN:], sem_g)
     for copy in rest_a:
         copy.wait_recv()
     share_a.append(share(place, wa_ref.at[0, 1:], wa_ref.at[1, 1:], sem_wa, 7))
@@ -471,7 +514,7 @@
     def forward(normed):
         gate = nn(w_gate, normed)
         hidden = (gate * jax.nn.sigmoid(gate) * nn(w_up, normed)).astype(BF16)
-        return tn(w_down, hidden)
+        return tn_narrow(w_down, hidden)
 
     z = forward(na_ref[:, :OWN])
     pass_on(fetch_b, wb_ref.at[0, 1:4, rows(x, 96)], sem_wb, 3, rest_b)
@@ -515,11 +558,11 @@
     share_b.append(share(place, wb_ref.at[0, 1:], wb_ref.at[1, 1:], sem_wb, 7))
     for copy in fetch_a + fetch_b + fetch_t + rest_a + rest_t + share_a + [share_t] + first + second + sends:
         copy.wait_send()
-    move_go.wait()
     move_n.wait_send()
     move_z.wait_send()
-    spread_n3, forward_n3, close_n3 = gather_all(place, n3_all, sem_all)
-    spread_n3()
+    gather_n3 = Gather(place, n3_all, sem_all)
+    gather_n3.begin()
+    move_go = swap(place, go2.at[:, :OWN], go2.at[:, OWN:], sem_g)
     spread(qkv_ref, keys, values)
     for part in range(2):
         quarter = place.quarters[part]
@@ -557,6 +600,7 @@
         def _():
             all_heads[chip] = own_heads[slot]
 
+    gather_n3.relay()
     arrivals = [
         remote(own_heads.at[0], all_heads.at[head], sem_o, head, place.partner) for head in range(CHIPS)
     ]
@@ -564,12 +608,12 @@
         pl.when(head * 2 + place.query_core != me)(arrivals[head].wait_recv)
     w_out = wat_ref[:, :, 3 * CH :].reshape(D, D)
     outputs = all_heads[...].reshape(D, OWN)
-    x3 = x2 + tn(w_out, outputs)
+    x3 = x2 + tn_narrow(w_out, outputs)
     x3_ref[...] = x3
     gain_b = gains_all[:, 2:3].astype(F32)
     nb[:, :OWN] = norm_forward(x3, gain_b)[0].astype(BF16)
     move_n = swap(place, nb.at[:, :OWN], nb.at[:, OWN:], sem_nb)
-    for copy in share_b:
+    for copy in share_b + [move_go]:
         copy.wait_recv()
     weights = hidden_weights(wb_ref)
     normed_grad = hidden_backward(weights, nb[:, :OWN], go2[:, :OWN], acts, slice(0, OWN))
@@ -583,9 +627,9 @@
         share(place, nb, nb_got, sem_act, 1),
         share(place, go2, go_got, sem_act, 2),
     ]
-    parts_z[...] = tn(weights[2], acts[2, :, OWN:]).astype(BF16)
+    parts_z[...] = tn_narrow(weights[2], acts[2, :, OWN:]).astype(BF16)
     move_z = swap(place, parts_z, got_z, sem_zb)
-    z = tn(weights[2], acts[2, :, :OWN])
+    z = tn_narrow(weights[2], acts[2, :, :OWN])
     move_gn.wait_recv()
     normed_grad = normed_grad + got_n[...].astype(F32)
     stream_grad, gain_grad = norm_backward(normed_grad, x3_ref[...], gain_b)
@@ -619,7 +663,8 @@
         copy.start()
         moves.append(copy)
     out_ref[:, half(me)] = out_own[rows(me, CH), :]
-    forward_n3()
+    for index in range(3):
+        gather_n3.arrive(index)
     gwo_ref[...] = nt(outputs, gy).astype(BF16).reshape(MP, CH, D)
     for copy in shares:
         copy.wait_recv()
@@ -632,8 +677,10 @@
         pl.when(slot_out * 2 + place.query_core != me)(sends[slot_out].wait_send)
     for copy in moves:
         copy.wait()
-    close_n3()
-    for copy in rest_b + share_b + shares + [move_n, move_gn, move_z]:
+    for index in range(-1, 3):
+        gather_n3.joined(index)
+    gather_n3.close()
+    for copy in rest_b + share_b + shares + [move_go, move_n, move_gn, move_z]:
         copy.wait_send()
     for copy in saves:
         copy.wait()
@@ -715,13 +762,13 @@
 def second_kernel(
     pick_ref, x_ref, scale_ref, feat_in, x1_ref, x2_ref, na_ref, qkv_ref, wa_in, wat_in, gains_all,
     lse_ref, of_ref, go_heads, gx3_ref, n3_in, gwo_ref, gmlp_b, ggain_b, gains_ref, taps_ref, weight_in,
-    gx_ref, joint_ref, sum_a, sum_b, gain_sum,
+    gx_ref, joint_ref, sum_t, sum_a, sum_b, gain_sum,
     feat_ref, wa_ref, wat_ref, n3_all, weight_ref,
     keys, values, kv_grad, q_grad, mine, core_got, chip_sum, head_grads, gz, gz_got, na_got, parts, got,
     acts, acts_got, gy1_ref, row_got, q_rows, gwo_got,
-    bx_got, bx_sum, by_got, by_sum, bz_got, gmlp_a, ax_got, ax_sum, ay_got, ay_sum, az_got, ggain_ref, gain_got, gain_own, gain_dp,
-    reverse, table, feature_grad, shifted, total, gh_ref, joint, joint_got, inner,
-    sem_q, sem_n, sem_z, sem_y, sem_gwo, sem_rows, sem_b, sem_a, sem_g, sem_gd, sem_j, sem_jg, sem_p, sem_act, sem_load,
+    b_1, b_2, b_3, b_4, b_5, gmlp_a, a_1, a_2, a_3, a_4, a_5, a_6, a_7, a_8, a_9, a_10, gat, gat_got, ggain_ref, gain_got, gain_own, gain_dp,
+    reverse, table, feature_grad, shifted, total, gh_ref, joint_sum, joint, joint_got, inner,
+    sem_q, sem_n, sem_z, sem_y, sem_gwo, sem_rows, sem_b, sem_a, sem_a2, sem_t, sem_tg, sem_g, sem_gd, sem_j, sem_jg, sem_p, sem_act, sem_load,
 ):
     place = Place()
     me, dp, chip, core = place.me, place.dp, place.chip, place.core
@@ -734,22 +781,17 @@
         copy = pltpu.make_async_copy(src, dst, sem_load.at[len(loads)])
         copy.start()
         loads.append(copy)
-    greet(
+    arrived = greet(
         [place.around(step) for step in range(1, MP)]
         + [{"dp": place.along_dp(step)} for step in range(1, DP)]
     )
     gain_a = gains_all[:, 0:1].astype(F32)
     gain_n = gains_all[:, 1:2].astype(F32)
-    sum_of_b = GradientSum(place, gmlp_b, sum_b, (bx_got, bx_sum, by_got, by_sum, bz_got), sem_b)
-    sum_of_a = GradientSum(place, gmlp_a, sum_a, (ax_got, ax_sum, ay_got, ay_sum, az_got), sem_a)
-    share_n = share(place, na_ref, na_got, sem_act, 0)
-    sum_of_b.over_x()
-    o_first = []
-    for step in range(1, MP):
-        there = place.around(step)
-        copy = remote(gwo_ref.at[there], gwo_got.at[step - 1], sem_gwo, step - 1, there)
-        copy.start()
-        o_first.append(copy)
+    sum_of_b = GradientSum(place, gmlp_b, sum_b, (b_1, b_2, b_3, b_4, b_5), sem_b, 0, 48, False)
+    sums_of_a = (
+        GradientSum(place, gmlp_a, sum_a, (a_1, a_2, a_3, a_4, a_5), sem_a, 0, 32, False),
+        GradientSum(place, gmlp_a, sum_a, (a_6, a_7, a_8, a_9, a_10), sem_a2, 256, 16, True),
+    )
     pick = pick_ref[0]
     spread(qkv_ref, keys, values)
     for part in range(2):
@@ -773,6 +815,16 @@
                 both = both + kv_grad[here]
             kv_grad[here] = both
         q_grad[part] = (query_grad * HD**-0.5).astype(BF16)
+        if part == 0:
+            arrived()
+            share_n = share(place, na_ref, na_got, sem_act, 0)
+            sum_of_b.first()
+            o_first = []
+            for step in range(1, MP):
+                there = place.around(step)
+                copy = remote(gwo_ref.at[there], gwo_got.at[step - 1], sem_gwo, step - 1, there)
+                copy.start()
+                o_first.append(copy)
     for index in range(MP):
         mine[index // 2, index % 2, :HD] = jnp.zeros((HD, OWN), BF16)
         mine[index // 2, index % 2, HD:] = kv_grad[index * OWN : (index + 1) * OWN].T.astype(BF16)
@@ -805,13 +857,13 @@
     loads[0].wait()
     w_qkv = wat_ref[:, :, : 3 * CH].reshape(3 * D, D)
     columns = head_grads[...].reshape(3 * D, OWN)
-    stream_grad, gain_grad = norm_backward(tn(w_qkv, columns), x2_ref[...], gain_n)
+    stream_grad, gain_grad = norm_backward(tn_narrow(w_qkv, columns), x2_ref[...], gain_n)
     lane = lax.broadcasted_iota(jnp.int32, (D, OWN), 1)
     gain_grads = jnp.where(lane == 1, gain_grad, 0.0) + jnp.where(lane == 2, ggain_b[...], 0.0)
     gx2 = gx3_ref[...] + stream_grad
     gz[:, :OWN] = gx2.astype(BF16)
     move_gz = swap(place, gz.at[:, :OWN], gz.at[:, OWN:], sem_n)
-    sum_of_b.over_y()
+    sum_of_b.second()
     loads[1].wait()
     weights = hidden_weights(wa_ref)
     normed_grad = hidden_backward(weights, na_ref[:, :OWN], gz[:, :OWN], acts, slice(0, OWN))
@@ -825,32 +877,39 @@
         share(place, acts.at[:, D:], acts_got, sem_act, 1),
         share(place, gz, gz_got, sem_act, 2),
     ]
-    sum_of_b.over_z()
+    sum_of_b.third()
     for copy in shares:
         copy.wait_recv()
     hidden_weight_grads(acts, acts_got, ((na_ref, na_got), (na_ref, na_got), (gz, gz_got)), gmlp_a)
-    sum_of_a.over_x()
+    for part in sums_of_a:
+        part.first()
     move_gn.wait_recv()
     normed_grad = normed_grad + got[...].astype(F32)
     stream_grad, gain_grad = norm_backward(normed_grad, x1_ref[...], gain_a)
     ggain_ref[...] = gain_grads + jnp.where(lane == 0, gain_grad, 0.0)
     gy1_ref[:, half(me)] = (gx2 + stream_grad).astype(BF16)
-    spread_gy1, forward_gy1, close_gy1 = gather_all(place, gy1_ref, sem_y)
-    spread_gy1()
+    gather_gy1 = Gather(place, gy1_ref, sem_y)
+    gather_gy1.begin()
     sum_of_b.back()
     share_q.wait_recv()
     loads[2].wait()
     for index in range(CHIPS):
         q_rows[:, half(index * 2 + core)] = chip_sum[index, rows(core, 96), :]
         q_rows[:, half(index * 2 + 1 - core)] = row_got[index]
-    joint[FEAT : FEAT + 3 * CH] = nt(q_rows[...], n3_all[...]).astype(BF16)
+    gat[: 3 * CH] = nt(q_rows[...], n3_all[...]).astype(BF16)
     for copy in o_first:
         copy.wait_recv()
     value = gwo_ref[me].astype(F32)
     for index in range(MP - 1):
         value = value + gwo_got[index].astype(F32)
-    joint[FEAT + 3 * CH : FEAT + OWN] = value.astype(BF16)
-    joint[FEAT + OWN :] = jnp.zeros((CH, D), BF16)
+    gat[3 * CH :] = value.astype(BF16)
+    t_first = []
+    for step in range(1, DP):
+        there = place.along_dp(step)
+        copy = remote(gat.at[rows(there, 16)], gat_got.at[step - 1], sem_t, step - 1, {"dp": there})
+        copy.start()
+        t_first.append(copy)
+    gather_gy1.relay()
     reverse_taps(taps_ref, reverse)
 
     def build(filter_index, slot):
@@ -859,30 +918,51 @@
 
         toeplitz_down(reverse[pl.ds(filter_index, 1), :], store)
 
-    @pl.loop(0, K // 2)
-    def _(index):
-        build(index, index)
-
-    forward_gy1()
-    close_gy1()
+    def build_some(begin, end):
+        @pl.loop(begin, end)
+        def _(index):
+            build(index, index)
+
+    joint_sum[...] = jnp.zeros_like(joint_sum)
+
+    def absorb(quarter):
+        here = pl.ds(pl.multiple_of(quarter * 512, 512), 512)
+        grads = gy1_ref[:, here]
+        joint_sum[...] += nt(feat_ref[:, here], grads)
+        feature_grad[:, here] = nn(weight_ref[: K * CH], grads).astype(BF16)
+
+    loads[3].wait()
+    loads[4].wait()
+    build_some(0, 4)
+    gather_gy1.joined(-1)
+    absorb(place.z)
+    gather_gy1.arrive(0)
+    build_some(4, 8)
+    gather_gy1.joined(0)
+    absorb((place.z + 3) % 4)
+    gather_gy1.arrive(1)
+    build_some(8, K // 2)
+    gather_gy1.joined(1)
+    absorb((place.z + 1) % 4)
+    gather_gy1.arrive(2)
+    for part in sums_of_a:
+        part.second()
+    gather_gy1.joined(2)
+    absorb((place.z + 2) % 4)
     gain_first = []
     for step in range(1, MP):
         there = place.around(step)
         copy = remote(ggain_ref.at[rows(there, CH)], gain_got.at[step - 1], sem_g, step - 1, there)
         copy.start()
         gain_first.append(copy)
-    loads[3].wait()
-    loads[4].wait()
-    joint[:FEAT] = nt(feat_ref[...], gy1_ref[...]).astype(BF16)
+    joint[:FEAT] = joint_sum[...].astype(BF16)
+    joint[FEAT:] = jnp.zeros((CH, D), BF16)
     j_first = []
     for step in range(1, DP):
         there = place.along_dp(step)
-        copy = remote(joint.at[rows(there, OWN)], joint_got.at[step - 1], sem_j, step - 1, {"dp": there})
+        copy = remote(joint.at[rows(there, 112)], joint_got.at[step - 1], sem_j, step - 1, {"dp": there})
         copy.start()
         j_first.append(copy)
-    for group in range(4):
-        here = slice(group * 512, (group + 1) * 512)
-        feature_grad[:, here] = nn(weight_ref[: K * CH], gy1_ref[:, here]).astype(BF16)
     total[...] = jnp.zeros_like(total)
     shifted[...] = jnp.zeros_like(shifted)
     joined = jnp.full((CH, T // 2), (pick == 1).astype(F32)).astype(BF16)
@@ -902,13 +982,25 @@
         total[:middle] += nn(shifted[:middle, :], table[slot])
         total[middle:] += nn(shifted[middle:, : T // 2], table[slot, : T // 2, :])
 
-    sum_of_a.over_y()
 
     @pl.loop(0, K // 2)
     def _(index):
         convolve(index, index)
 
-    sum_of_a.over_z()
+    for part in sums_of_a:
+        part.third()
+    last = []
+    for copy in t_first:
+        copy.wait_recv()
+    value = gat[rows(dp, 16), :].astype(F32)
+    for index in range(DP - 1):
+        value = value + gat_got[index].astype(F32)
+    sum_t[rows(dp, 16), :] = value.astype(BF16)
+    done_t = sum_t.at[rows(dp, 16)]
+    for step in range(1, DP):
+        copy = remote(done_t, done_t, sem_tg, step - 1, {"dp": place.along_dp(step)})
+        copy.start()
+        last.append(copy)
 
     @pl.loop(K // 2, K)
     def _(index):
@@ -932,7 +1024,6 @@
         copy = remote(inner.at[me], inner.at[me], sem_p, step - 1, place.around(step))
         copy.start()
         sums.append(copy)
-    last = []
     scaling = scale_ref[...]
     gain_grad = jnp.sum(gh_ref[...] * stream * scaling, axis=1, keepdims=True)
     for copy in gain_first:
@@ -948,16 +1039,17 @@
         last.append(copy)
     for copy in j_first:
         copy.wait_recv()
-    value = joint[rows(dp, OWN), :].astype(F32)
+    value = joint[rows(dp, 112), :].astype(F32)
     for index in range(DP - 1):
         value = value + joint_got[index].astype(F32)
-    joint_ref[rows(dp, OWN), :] = value.astype(BF16)
-    done_j = joint_ref.at[rows(dp, OWN)]
+    joint_ref[rows(dp, 112), :] = value.astype(BF16)
+    done_j = joint_ref.at[rows(dp, 112)]
     for step in range(1, DP):
         copy = remote(done_j, done_j, sem_jg, step - 1, {"dp": place.along_dp(step)})
         copy.start()
         last.append(copy)
-    sum_of_a.back()
+    for part in sums_of_a:
+        part.back()
     for copy in sums:
         copy.wait()
     value = inner[0]
@@ -971,9 +1063,11 @@
     for index in range(DP - 1):
         value = value + gain_dp[index]
     gain_sum[...] = value
-    for copy in first + second + [share_q] + shares + [move_gz, move_gn] + o_first + j_first + gain_first:
+    for copy in first + second + [share_q] + shares + [move_gz, move_gn] + o_first + t_first + j_first + gain_first:
         copy.wait_send()
-    sum_of_a.close()
+    gather_gy1.close()
+    for part in sums_of_a:
+        part.close()
     sum_of_b.close()
 
 
@@ -982,7 +1076,8 @@
         second_kernel,
         out_shape=(
             jax.ShapeDtypeStruct((CH, T), F32),
-            jax.ShapeDtypeStruct((DP * OWN, D), BF16),
+            jax.ShapeDtypeStruct((DP * 112, D), BF16),
+            jax.ShapeDtypeStruct((OWN, D), BF16),
             jax.ShapeDtypeStruct((3 * OWN, D), BF16),
             jax.ShapeDtypeStruct((3 * OWN, D), BF16),
             jax.ShapeDtypeStruct((CH, OWN), F32),
@@ -992,7 +1087,7 @@
         + [ANY]
         + [VMEM] * 5
         + [ANY],
-        out_specs=(VMEM,) * 5,
+        out_specs=(VMEM,) * 6,
         scratch_shapes=[
             pltpu.VMEM((FEAT, T), BF16),
             pltpu.VMEM((2, 4, 3 * OWN, D), BF16),
@@ -1018,17 +1113,12 @@
             pltpu.VMEM((CHIPS, 96, OWN), BF16),
             pltpu.VMEM((96, T), BF16),
             pltpu.VMEM((MP - 1, CH, D), BF16),
-            pltpu.VMEM((3, 4, 96, D), BF16),
-            pltpu.VMEM((4, 96, D), BF16),
-            pltpu.VMEM((4, 48, D), BF16),
-            pltpu.VMEM((4, 48, D), BF16),
-            pltpu.VMEM((3, 48, D), BF16),
+            *sum_buffers(48, False),
             pltpu.VMEM((4, 3 * OWN, D), BF16),
-            pltpu.VMEM((3, 4, 96, D), BF16),
-            pltpu.VMEM((4, 96, D), BF16),
-            pltpu.VMEM((4, 48, D), BF16),
-            pltpu.VMEM((4, 48, D), BF16),
-            pltpu.VMEM((3, 48, D), BF16),
+            *sum_buffers(32, False),
+            *sum_buffers(16, True),
+            pltpu.VMEM((OWN, D), BF16),
+            pltpu.VMEM((DP - 1, 16, D), BF16),
             pltpu.VMEM((D, OWN), F32),
             pltpu.VMEM((MP - 1, CH, OWN), F32),
             pltpu.VMEM((CH, OWN), F32),
@@ -1039,10 +1129,11 @@
             pltpu.VMEM((CH * T // (2 * OWN), T), BF16),
             pltpu.VMEM((CH * T // (2 * OWN), 2 * OWN), F32),
             pltpu.VMEM((CH, T), F32),
-            pltpu.VMEM((DP * OWN, D), BF16),
-            pltpu.VMEM((DP - 1, OWN, D), BF16),
+            pltpu.VMEM((FEAT, D), F32),
+            pltpu.VMEM((DP * 112, D), BF16),
+            pltpu.VMEM((DP - 1, 112, D), BF16),
             pltpu.VMEM((MP, 1, T), F32),
-            sems(15), sems(1), sems(1), sems(15), sems(15), sems(1), sems(14), sems(14), sems(15),
+            sems(15), sems(1), sems(1), sems(15), sems(15), sems(1), sems(14), sems(14), sems(14), sems(7), sems(7), sems(15),
             sems(7), sems(7), sems(7), sems(15), sems(3),
             pltpu.SemaphoreType.DMA((5,)),
         ],
@@ -1054,12 +1145,12 @@
 
 
 def final_kernel(
-    joint_ref, a_ref, b_ref, gain_ref,
+    joint_ref, t_ref, a_ref, b_ref, gain_ref,
     gws, gate_ga, up_ga, down_ga, gqkv, gout, gate_gb, up_gb, down_gb, *gain_grads,
 ):
     gws[...] = joint_ref[:FEAT].astype(F32)
-    gqkv[...] = joint_ref[FEAT : FEAT + 3 * CH].astype(F32)
-    gout[...] = joint_ref[FEAT + 3 * CH : FEAT + OWN].astype(F32)
+    gqkv[...] = t_ref[: 3 * CH].astype(F32)
+    gout[...] = t_ref[3 * CH :].astype(F32)
     for ref, (gate, up, down) in ((a_ref, (gate_ga, up_ga, down_ga)), (b_ref, (gate_gb, up_gb, down_gb))):
         gate[...] = ref[:OWN].astype(F32).T
         up[...] = ref[OWN : 2 * OWN].astype(F32).T
@@ -1081,7 +1172,7 @@
             *mlp,
             *[jax.ShapeDtypeStruct((1, CH), F32)] * 4,
         ),
-        in_specs=[VMEM] * 4,
+        in_specs=[VMEM] * 5,
         out_specs=(VMEM,) * 13,
         compiler_params=pltpu.CompilerParams(vmem_limit_bytes=LIMIT),
         name="final",
@@ -1104,11 +1195,11 @@
         shape_pick, x, out_grad.T, gains, filters, weight,
         gate_a, up_a, down_a, qkv_weight.T, out_weight, gate_b, up_b, down_b,
     )
-    gx, joint, ga, gb, gain_sum = second(
+    gx, joint, gat, ga, gb, gain_sum = second(
         shape_pick, x, scaling, features, x1, x2, na, qkv, wa, wat, gains_all,
         lse, of, go_heads, gx3, n3_all, gwo, gmlp_b, ggain_b, gains, filters, weight,
     )
-    gws, gate_ga, up_ga, down_ga, gqkv, gout, gate_gb, up_gb, down_gb, *gain_grads = final(joint, ga, gb, gain_sum)
+    gws, gate_ga, up_ga, down_ga, gqkv, gout, gate_gb, up_gb, down_gb, *gain_grads = final(joint, gat, ga, gb, gain_sum)
     gain_a, gain_n, gain_b, gain_s = (grad.reshape(CH) for grad in gain_grads)
     return (
         out.T, gx.T, gain_s, gws.reshape(K + LAGS, CH, D), gain_a, gate_ga, up_ga, down_ga,

time: 223 us -> 210 us (0.942)
  Pallas kernels: 218 us -> 205 us
    pallas_call x1, Pallas kernels: 109 us -> 101 us  [first(): pl.pallas_call(first_kernel, out_shape=(jax.ShapeDtypeStruct((1, T), F32)...]
    pallas_call x1, Pallas kernels: 106 us -> 100 us  [second(): pl.pallas_call(second_kernel, out_shape=(jax.ShapeDtypeStruct((CH, T), F3...]
where the time goes in v1:
time: 210 us; the launch traced here: 209 us
  Pallas kernels  205 us (98%)
    pallas_call x1, Pallas kernels, first(): pl.pallas_call(first_kernel, out_shape=(jax.ShapeDtypeStruct((1, T), F32)...  101 us
    pallas_call x1, Pallas kernels, second(): pl.pallas_call(second_kernel, out_shape=(jax.ShapeDtypeStruct((CH, T), F3...  100 us

profile of v1, /device:TPU:0, one launch (start us, length us, event | category | flops | bytes accessed | tf_op | source)
XLA Modules:
  0.0 208.9 jit_solution(6908880227907018026)
XLA Ops:
  1.3 0.7 pad_maximum_fusion
  2.0 0.1 copy.36
  2.1 0.6 pad.4.gains_ref
  2.7 101.0 %first.1 = (f32[1,2048]{1,0:T(1,128)}, bf16[864,2048]{1,0:T(8,128)(2,1)}, f32[512,128]{1,0:T(8,128)}, f32[512,128]{1,0:T(8,128)}, bf16[512,256]{1,0:T(8,128)(2,1...) custom-call(s32[1]{0:T(128)S(6)} %copy.39.pick_ref, ...), custom_call_target="tpu_custom_call" | custom-call | tf_op jit(solution)/shard_map/first/pallas_call | solution.py:690
  103.7 0.0 copy-start.1
  103.7 100.4 %second.1 = (f32[32,2048]{1,0:T(8,128)}, bf16[896,512]{1,0:T(8,128)(2,1)}, bf16[128,512]{1,0:T(8,128)(2,1)}, bf16[384,512]{1,0:T(8,128)(2,1)}, bf16[384,512]{1,0:T(8,128)(2,1)}, /*index=5*/f32[32,128]{1,0:T(8,128)}) custom-call(s32[1]{0:T(128)S(6)} %copy.39.pick_ref, bf16[32,2048]{1,0:T(8,128)(2,1)} %bitcast.19, f32[1,2048]{1,0:T(1,128)} %get-tuple-element.53.scale_ref, ...), custom_call_target="tpu_custom_call" | custom-call | tf_op jit(solution)/shard_map/second/pallas_call | solution.py:1075
  204.1 0.0 copy-start
  204.1 3.5 %final.1 = (f32[864,512]{1,0:T(8,128)}, f32[512,128]{1,0:T(8,128)}, f32[512,128]{1,0:T(8,128)}, f32[128,512]{1,0:T(8,128)}, f32[96,512]{1,0:T(8,128)}, /*index=5...) custom-call(bf16[896,512]{1,0:T(8,128)(2,1)} %get-tuple-element.71.j, ...), custom_call_target="tpu_custom_call" | custom-call | tf_op jit(solution)/shard_map/final/pallas_call | solution.py:1165
  207.6 0.0 copy-done.1
  207.6 0.7 copy.40
  208.2 0.0 copy-done
  208.2 0.7 copy.41
Async XLA Ops:
  103.7 103.9 %copy-start.1 = (bf16[32,2048]{1,0:T(8,128)(2,1)S(1)}, bf16[32,2048]{1,0:T(8,128)(2,1)}, u32[]{:S(2)}) copy-start(bf16[32,2048]{1,0:T(8,128)(2,1)} %get-tuple-element.52) | copy-start | bytes 393220
  204.1 4.1 %copy-start = (f32[32,2048]{1,0:T(8,128)S(1)}, f32[32,2048]{1,0:T(8,128)}, u32[]{:S(2)}) copy-start(f32[32,2048]{1,0:T(8,128)} %get-tuple-element.70) | copy-start | bytes 786436

commit v2 on v1

--- a/solution.py
+++ b/solution.py
@@ -337,12 +337,12 @@
     pick_ref, x_ref, go_ref, gains_ref, taps_ref, weight_ref,
     gate_a, up_a, down_a, qkv_w, out_w, gate_b, up_b, down_b,
     scale_ref, feat_out, x1_ref, x2_ref, na_out, qkv_out, wa_out, wat_out, gains_all,
-    lse_ref, of_ref, go_heads, gx3_ref, out_ref, n3_all, gwo_ref, gmlp_ref, ggain_ref,
-    feat_ref, na_ref, qkv_ref, wa_ref, wat_ref, x_own, go2, squares, taps, table, weight_t, blocks, y_ref,
+    lse_ref, of_ref, go_heads, gx3_ref, out_ref, n3_ref, gwo_ref, gmlp_ref, ggain_ref,
+    feat_ref, na_ref, qkv_ref, wa_ref, wat_ref, streams, streams_own, go2, squares, taps, table, table_late, weight_t, blocks, y_ref,
     core_got, chip_got, parts, got, heads, wb_ref, keys, values, own_heads, all_heads, x3_ref, nb, nb_got, go_got,
     acts, acts_got, parts_n, got_n, parts_z, got_z, grad_heads, out_own,
-    sem_s, sem_x, sem_go, sem_gain, sem_wa, sem_wb, sem_wat, sem_y, sem_n, sem_g, sem_z, sem_q,
-    sem_o, sem_nb, sem_gn, sem_zb, sem_h, sem_out, sem_all, sem_act, sem_save,
+    sem_s, sem_x, sem_wa, sem_wb, sem_wat, sem_y, sem_n, sem_g, sem_z, sem_q,
+    sem_o, sem_nb, sem_gn, sem_zb, sem_h, sem_out, sem_act, sem_save,
 ):
     place = Place()
     me, chip, core, x = place.me, place.chip, place.core, place.x
@@ -359,17 +359,23 @@
         ref[0, 0, :OWN] = gate[...].T
         ref[0, 0, OWN : 2 * OWN] = up[...].T
         ref[0, 0, 2 * OWN :] = down[...]
+    streams[0] = x_ref[...]
+    streams[1] = go_ref[...]
+    for index in range(MP):
+        streams[2, :, index * OWN : (index + 1) * OWN] = gains_ref[...]
+    streams_own[:, rows(me, CH)] = streams[:, :, half(me)]
     taps[...] = taps_ref[...].astype(F32)
 
-    def build(step):
+    def build(step, table, shift=0):
         for index in range(2):
-            filter_table = toeplitz(taps[pl.ds(step * 2 + index, 1), :])
+            filter_table = toeplitz(taps[pl.ds((step + shift) * 2 + index, 1), :])
             for offset in range(count):
                 table[step, offset * OWN : (offset + 1) * OWN, index * OWN : (index + 1) * OWN] = filter_table[
                     :, offset * OWN : (offset + 1) * OWN
                 ]
 
-    pl.loop(0, EARLY_TABLES)(build)
+    build_early = lambda step: build(step, table)
+    pl.loop(0, EARLY_TABLES)(build_early)
     arrived()
     sums, late, fetch_a, fetch_b, fetch_t, rest_a, rest_b, rest_t = [], [], [], [], [], [], [], []
     for step in range(1, MP):
@@ -390,14 +396,11 @@
         fetch_t.append(copy)
     for step in range(1, MP):
         there = place.around(step)
-        for src, dst, sem in (
-            (x_ref.at[:, half(there)], x_own.at[rows(me, CH)], sem_x),
-            (go_ref.at[:, half(there)], go2.at[rows(me, CH), :OWN], sem_go),
-            (gains_ref, gains_all.at[rows(me, CH)], sem_gain),
-        ):
-            copy = remote(src, dst, sem, step - 1, there)
-            copy.start()
-            late.append(copy)
+        copy = remote(
+            streams.at[:, :, half(there)], streams_own.at[:, rows(me, CH)], sem_x, step - 1, there
+        )
+        copy.start()
+        late.append(copy)
     for step in range(1, 4):
         copy = remote(
             wb_ref.at[0, 0, rows(x, 96)], wb_ref.at[0, step, rows(x, 96)], sem_wb, step - 1, place.same_units(step)
@@ -406,11 +409,8 @@
         fetch_b.append(copy)
     share_a = [share(place, wa_ref.at[0, 0], wa_ref.at[1, 0], sem_wa, 6)]
     share_b = [share(place, wb_ref.at[0, 0], wb_ref.at[1, 0], sem_wb, 6)]
-    x_own[rows(me, CH), :] = x_ref[:, half(me)]
-    go2[rows(me, CH), :OWN] = go_ref[:, half(me)]
-    gains_all[rows(me, CH)] = gains_ref[...]
     weight_t[...] = weight_ref[...].T
-    pl.loop(EARLY_TABLES, K // 2)(build)
+    pl.loop(EARLY_TABLES, K // 4)(build_early)
     for copy in sums:
         copy.wait()
     total = squares[0]
@@ -438,11 +438,11 @@
         moved = jnp.where(lag_mask(shift, pick), moved, 0.0).astype(BF16)
         feat_ref[(K + shift) * CH : (K + shift + 1) * CH, :] = moved
 
-    def convolve(step):
+    def convolve(step, table, shift=0):
         early = nn(blocks[: CH * count // 2, : T // 2], table[step, : T // 2, :]).astype(BF16)
         late_half = nn(blocks[CH * count // 2 :, :], table[step]).astype(BF16)
         for index in range(2):
-            base = pl.multiple_of((step * 2 + index) * CH, CH)
+            base = pl.multiple_of(((step + shift) * 2 + index) * CH, CH)
             for target in range(count):
                 part, at = (early, target) if target < count // 2 else (late_half, target - count // 2)
                 feat_ref[pl.ds(base, CH), target * OWN : (target + 1) * OWN] = part[
@@ -458,9 +458,17 @@
             copy.start()
             rest.append(copy)
 
-    pl.loop(0, K // 4)(convolve)
+    @pl.loop(0, K // 4)
+    def _(step):
+        build(step, table_late, K // 4)
+        convolve(step, table)
+
     pass_on(fetch_a, wa_ref.at[0, 1:4, rows(x, 96)], sem_wa, 3, rest_a)
-    pl.loop(K // 4, K // 2)(convolve)
+
+    @pl.loop(0, K // 4)
+    def _(step):
+        convolve(step, table_late, K // 4)
+
     saves = []
 
     def save(src, dst):
@@ -494,12 +502,15 @@
     pass_on(fetch_t, wat_ref.at[:, core, rows(x, CH)], sem_wat, 7, rest_t)
     for copy in late:
         copy.wait()
+    go2[:, :OWN] = streams_own[1]
+    move_go = swap(place, go2.at[:, :OWN], go2.at[:, OWN:], sem_g)
+    gains_all[...] = streams_own[2]
     for copy in rest_a:
         copy.wait_recv()
     share_a.append(share(place, wa_ref.at[0, 1:], wa_ref.at[1, 1:], sem_wa, 7))
     for move in second:
         move.wait_recv()
-    x1 = x1_ref[...] + x_own[...].astype(F32)
+    x1 = x1_ref[...] + streams_own[0].astype(F32)
     for index in range(CHIPS - 1):
         x1 = x1 + chip_got[index].astype(F32)
     x1_ref[...] = x1
@@ -530,7 +541,7 @@
     x2 = x1 + z + got[...].astype(F32)
     x2_ref[...] = x2
     n3 = norm_forward(x2, gains_all[:, 1:2].astype(F32))[0].astype(BF16)
-    n3_all[:, half(me)] = n3
+    n3_ref[...] = n3
     share_t.wait_recv()
     save(wat_ref, wat_out)
     w_qkv = wat_ref[:, :, : 3 * CH].reshape(3 * D, D)
@@ -560,9 +571,6 @@
         copy.wait_send()
     move_n.wait_send()
     move_z.wait_send()
-    gather_n3 = Gather(place, n3_all, sem_all)
-    gather_n3.begin()
-    move_go = swap(place, go2.at[:, :OWN], go2.at[:, OWN:], sem_g)
     spread(qkv_ref, keys, values)
     for part in range(2):
         quarter = place.quarters[part]
@@ -600,7 +608,6 @@
         def _():
             all_heads[chip] = own_heads[slot]
 
-    gather_n3.relay()
     arrivals = [
         remote(own_heads.at[0], all_heads.at[head], sem_o, head, place.partner) for head in range(CHIPS)
     ]
@@ -663,8 +670,6 @@
         copy.start()
         moves.append(copy)
     out_ref[:, half(me)] = out_own[rows(me, CH), :]
-    for index in range(3):
-        gather_n3.arrive(index)
     gwo_ref[...] = nt(outputs, gy).astype(BF16).reshape(MP, CH, D)
     for copy in shares:
         copy.wait_recv()
@@ -677,9 +682,6 @@
         pl.when(slot_out * 2 + place.query_core != me)(sends[slot_out].wait_send)
     for copy in moves:
         copy.wait()
-    for index in range(-1, 3):
-        gather_n3.joined(index)
-    gather_n3.close()
     for copy in rest_b + share_b + shares + [move_go, move_n, move_gn, move_z]:
         copy.wait_send()
     for copy in saves:
@@ -704,7 +706,7 @@
             jax.ShapeDtypeStruct((8, HD, OWN), BF16),
             jax.ShapeDtypeStruct((D, OWN), F32),
             jax.ShapeDtypeStruct((CH, T), BF16),
-            jax.ShapeDtypeStruct((D, T), BF16),
+            jax.ShapeDtypeStruct((D, OWN), BF16),
             jax.ShapeDtypeStruct((MP, CH, D), BF16),
             jax.ShapeDtypeStruct((4, 3 * OWN, D), BF16),
             jax.ShapeDtypeStruct((D, 1), F32),
@@ -717,11 +719,13 @@
             pltpu.VMEM((MP, 3 * HD, OWN), BF16),
             pltpu.VMEM((2, 4, 3 * OWN, D), BF16),
             pltpu.VMEM((CHIPS, 2, OWN, D), BF16),
-            pltpu.VMEM((D, OWN), BF16),
+            pltpu.VMEM((3, CH, T), BF16),
+            pltpu.VMEM((3, D, OWN), BF16),
             pltpu.VMEM((D, 2 * OWN), BF16),
             pltpu.VMEM((MP, 1, T), F32),
             pltpu.VMEM((K, T), F32),
-            pltpu.VMEM((K // 2, T, 2 * OWN), BF16),
+            pltpu.VMEM((K // 4, T, 2 * OWN), BF16),
+            pltpu.VMEM((K // 4, T, 2 * OWN), BF16),
             pltpu.VMEM((D, FEAT), BF16),
             pltpu.VMEM((CH * T // OWN, T), BF16),
             pltpu.VMEM((CHIPS, 2, D, OWN), BF16),
@@ -747,9 +751,9 @@
             pltpu.VMEM((D, OWN), BF16),
             pltpu.VMEM((CHIPS, HD, OWN), BF16),
             pltpu.VMEM((D, OWN), BF16),
-            sems(15), sems(15), sems(15), sems(15), sems(8), sems(8), sems(11),
+            sems(15), sems(15), sems(8), sems(8), sems(11),
             sems(15), sems(1), sems(1), sems(1), sems(15),
-            sems(8), sems(1), sems(1), sems(1), sems(8), sems(15), sems(15), sems(3),
+            sems(8), sems(1), sems(1), sems(1), sems(8), sems(15), sems(3),
             pltpu.SemaphoreType.DMA((5,)),
         ],
         compiler_params=pltpu.CompilerParams(
@@ -761,22 +765,23 @@
 
 def second_kernel(
     pick_ref, x_ref, scale_ref, feat_in, x1_ref, x2_ref, na_ref, qkv_ref, wa_in, wat_in, gains_all,
-    lse_ref, of_ref, go_heads, gx3_ref, n3_in, gwo_ref, gmlp_b, ggain_b, gains_ref, taps_ref, weight_in,
+    lse_ref, of_ref, go_heads, gx3_ref, n3_ref, gwo_ref, gmlp_b, ggain_b, gains_ref, taps_ref, weight_in,
     gx_ref, joint_ref, sum_t, sum_a, sum_b, gain_sum,
     feat_ref, wa_ref, wat_ref, n3_all, weight_ref,
     keys, values, kv_grad, q_grad, mine, core_got, chip_sum, head_grads, gz, gz_got, na_got, parts, got,
     acts, acts_got, gy1_ref, row_got, q_rows, gwo_got,
-    b_1, b_2, b_3, b_4, b_5, gmlp_a, a_1, a_2, a_3, a_4, a_5, a_6, a_7, a_8, a_9, a_10, gat, gat_got, ggain_ref, gain_got, gain_own, gain_dp,
+    b_1, b_2, b_3, b_4, b_5, gmlp_a, a_1, a_2, a_3, a_4, a_5, a_6, a_7, a_8, a_9, a_10, gat, gat_got, ggain_ref, gain_own, gain_dp,
     reverse, table, feature_grad, shifted, total, gh_ref, joint_sum, joint, joint_got, inner,
-    sem_q, sem_n, sem_z, sem_y, sem_gwo, sem_rows, sem_b, sem_a, sem_a2, sem_t, sem_tg, sem_g, sem_gd, sem_j, sem_jg, sem_p, sem_act, sem_load,
+    sem_q, sem_n, sem_z, sem_y, sem_gwo, sem_rows, sem_b, sem_a, sem_a2, sem_t, sem_tg, sem_gd, sem_j, sem_jg, sem_p, sem_act, sem_all, sem_load,
 ):
     place = Place()
     me, dp, chip, core = place.me, place.dp, place.chip, place.core
     wide = 2 * OWN
     count = T // wide
+    n3_all[:, half(me)] = n3_ref[...]
     loads = []
     for src, dst in (
-        (wat_in, wat_ref), (wa_in, wa_ref), (n3_in, n3_all), (feat_in, feat_ref), (weight_in, weight_ref)
+        (wat_in, wat_ref), (wa_in, wa_ref), (feat_in, feat_ref), (weight_in, weight_ref)
     ):
         copy = pltpu.make_async_copy(src, dst, sem_load.at[len(loads)])
         copy.start()
@@ -817,6 +822,8 @@
         q_grad[part] = (query_grad * HD**-0.5).astype(BF16)
         if part == 0:
             arrived()
+            gather_n3 = Gather(place, n3_all, sem_all)
+            gather_n3.begin()
             share_n = share(place, na_ref, na_got, sem_act, 0)
             sum_of_b.first()
             o_first = []
@@ -878,6 +885,7 @@
         share(place, gz, gz_got, sem_act, 2),
     ]
     sum_of_b.third()
+    gather_n3.relay()
     for copy in shares:
         copy.wait_recv()
     hidden_weight_grads(acts, acts_got, ((na_ref, na_got), (na_ref, na_got), (gz, gz_got)), gmlp_a)
@@ -891,8 +899,11 @@
     gather_gy1 = Gather(place, gy1_ref, sem_y)
     gather_gy1.begin()
     sum_of_b.back()
+    for index in range(3):
+        gather_n3.arrive(index)
     share_q.wait_recv()
-    loads[2].wait()
+    for index in range(-1, 3):
+        gather_n3.joined(index)
     for index in range(CHIPS):
         q_rows[:, half(index * 2 + core)] = chip_sum[index, rows(core, 96), :]
         q_rows[:, half(index * 2 + 1 - core)] = row_got[index]
@@ -931,8 +942,8 @@
         joint_sum[...] += nt(feat_ref[:, here], grads)
         feature_grad[:, here] = nn(weight_ref[: K * CH], grads).astype(BF16)
 
+    loads[2].wait()
     loads[3].wait()
-    loads[4].wait()
     build_some(0, 4)
     gather_gy1.joined(-1)
     absorb(place.z)
@@ -949,12 +960,6 @@
         part.second()
     gather_gy1.joined(2)
     absorb((place.z + 2) % 4)
-    gain_first = []
-    for step in range(1, MP):
-        there = place.around(step)
-        copy = remote(ggain_ref.at[rows(there, CH)], gain_got.at[step - 1], sem_g, step - 1, there)
-        copy.start()
-        gain_first.append(copy)
     joint[:FEAT] = joint_sum[...].astype(BF16)
     joint[FEAT:] = jnp.zeros((CH, D), BF16)
     j_first = []
@@ -1018,7 +1023,10 @@
         gh_ref[...] += value
     stream = x_ref[...].astype(F32)
     scaled = gh_ref[...] * gains_ref[:, 3:4].astype(F32)
-    inner[pl.ds(me, 1)] = jnp.sum(scaled * stream, axis=0, keepdims=True)[None]
+    partial = jnp.sum(scaled * stream, axis=0, keepdims=True)
+    for index in range(4):
+        inner[me, index : index + 1] = partial[:, index * 512 : (index + 1) * 512]
+    inner[me, 4:] = ggain_ref[...].T[:4]
     sums = []
     for step in range(1, MP):
         copy = remote(inner.at[me], inner.at[me], sem_p, step - 1, place.around(step))
@@ -1026,17 +1034,9 @@
         sums.append(copy)
     scaling = scale_ref[...]
     gain_grad = jnp.sum(gh_ref[...] * stream * scaling, axis=1, keepdims=True)
-    for copy in gain_first:
-        copy.wait_recv()
-    value = ggain_ref[rows(me, CH), :]
-    for index in range(MP - 1):
-        value = value + gain_got[index]
-    lane = lax.broadcasted_iota(jnp.int32, (CH, OWN), 1)
-    gain_own[...] = value + jnp.where(lane == 3, gain_grad, 0.0)
-    for step in range(1, DP):
-        copy = remote(gain_own, gain_dp.at[step - 1], sem_gd, step - 1, {"dp": place.along_dp(step)})
-        copy.start()
-        last.append(copy)
+    gain_grad = jnp.concatenate(
+        [jnp.broadcast_to(gain_grad, (CH, OWN)), jnp.zeros((OWN - CH, OWN), F32)], axis=0
+    ).T
     for copy in j_first:
         copy.wait_recv()
     value = joint[rows(dp, 112), :].astype(F32)
@@ -1055,6 +1055,13 @@
     value = inner[0]
     for index in range(1, MP):
         value = value + inner[index]
+    gain_own[...] = pltpu.roll(value, (D - CH * me) % D, 1)[:, :OWN]
+    gain_own[7:] = gain_grad[:1]
+    for step in range(1, DP):
+        copy = remote(gain_own, gain_dp.at[step - 1], sem_gd, step - 1, {"dp": place.along_dp(step)})
+        copy.start()
+        last.append(copy)
+    value = jnp.concatenate([value[index : index + 1] for index in range(4)], axis=1)
     stream_grad = scaled * scaling - stream * (scaling * scaling * scaling * value / D)
     gx_ref[...] = stream_grad + gy1_ref[rows(me, CH), :].astype(F32)
     for copy in last:
@@ -1063,8 +1070,9 @@
     for index in range(DP - 1):
         value = value + gain_dp[index]
     gain_sum[...] = value
-    for copy in first + second + [share_q] + shares + [move_gz, move_gn] + o_first + t_first + j_first + gain_first:
+    for copy in first + second + [share_q] + shares + [move_gz, move_gn] + o_first + t_first + j_first:
         copy.wait_send()
+    gather_n3.close()
     gather_gy1.close()
     for part in sums_of_a:
         part.close()
@@ -1080,13 +1088,9 @@
             jax.ShapeDtypeStruct((OWN, D), BF16),
             jax.ShapeDtypeStruct((3 * OWN, D), BF16),
             jax.ShapeDtypeStruct((3 * OWN, D), BF16),
-            jax.ShapeDtypeStruct((CH, OWN), F32),
+            jax.ShapeDtypeStruct((8, OWN), F32),
         ),
-        in_specs=[SMEM, VMEM, VMEM, ANY, VMEM, VMEM, VMEM, VMEM, ANY, ANY]
-        + [VMEM] * 5
-        + [ANY]
-        + [VMEM] * 5
-        + [ANY],
+        in_specs=[SMEM, VMEM, VMEM, ANY, VMEM, VMEM, VMEM, VMEM, ANY, ANY] + [VMEM] * 11 + [ANY],
         out_specs=(VMEM,) * 6,
         scratch_shapes=[
             pltpu.VMEM((FEAT, T), BF16),
@@ -1120,9 +1124,8 @@
             pltpu.VMEM((OWN, D), BF16),
             pltpu.VMEM((DP - 1, 16, D), BF16),
             pltpu.VMEM((D, OWN), F32),
-            pltpu.VMEM((MP - 1, CH, OWN), F32),
-            pltpu.VMEM((CH, OWN), F32),
-            pltpu.VMEM((DP - 1, CH, OWN), F32),
+            pltpu.VMEM((8, OWN), F32),
+            pltpu.VMEM((DP - 1, 8, OWN), F32),
             pltpu.VMEM((K, T + 2 * OWN), F32),
             pltpu.VMEM((K // 2, T, 2 * OWN), BF16),
             pltpu.VMEM((K * CH, T), BF16),
@@ -1132,10 +1135,10 @@
             pltpu.VMEM((FEAT, D), F32),
             pltpu.VMEM((DP * 112, D), BF16),
             pltpu.VMEM((DP - 1, 112, D), BF16),
-            pltpu.VMEM((MP, 1, T), F32),
-            sems(15), sems(1), sems(1), sems(15), sems(15), sems(1), sems(14), sems(14), sems(14), sems(7), sems(7), sems(15),
-            sems(7), sems(7), sems(7), sems(15), sems(3),
-            pltpu.SemaphoreType.DMA((5,)),
+            pltpu.VMEM((MP, 8, D), F32),
+            sems(15), sems(1), sems(1), sems(15), sems(15), sems(1), sems(14), sems(14), sems(14), sems(7), sems(7),
+            sems(7), sems(7), sems(7), sems(15), sems(3), sems(15),
+            pltpu.SemaphoreType.DMA((4,)),
         ],
         compiler_params=pltpu.CompilerParams(
             collective_id=1, has_side_effects=True, vmem_limit_bytes=LIMIT
@@ -1145,9 +1148,11 @@
 
 
 def final_kernel(
-    joint_ref, t_ref, a_ref, b_ref, gain_ref,
-    gws, gate_ga, up_ga, down_ga, gqkv, gout, gate_gb, up_gb, down_gb, *gain_grads,
+    joint_ref, t_ref, a_ref, b_ref, gain_ref, out_in, gx_in,
+    out_ref, gx_ref, gws, gate_ga, up_ga, down_ga, gqkv, gout, gate_gb, up_gb, down_gb, *gain_grads,
 ):
+    out_ref[...] = out_in[...]
+    gx_ref[...] = gx_in[...]
     gws[...] = joint_ref[:FEAT].astype(F32)
     gqkv[...] = t_ref[: 3 * CH].astype(F32)
     gout[...] = t_ref[3 * CH :].astype(F32)
@@ -1155,9 +1160,8 @@
         gate[...] = ref[:OWN].astype(F32).T
         up[...] = ref[OWN : 2 * OWN].astype(F32).T
         down[...] = ref[2 * OWN :].astype(F32)
-    columns = gain_ref[...].T
     for index, grad in enumerate(gain_grads):
-        grad[...] = columns[index : index + 1]
+        grad[...] = gain_ref[4 + index : 5 + index, :CH]
 
 
 def final(*operands):
@@ -1165,6 +1169,8 @@
     return pl.pallas_call(
         final_kernel,
         out_shape=(
+            jax.ShapeDtypeStruct((CH, T), BF16),
+            jax.ShapeDtypeStruct((CH, T), F32),
             jax.ShapeDtypeStruct((FEAT, D), F32),
             *mlp,
             jax.ShapeDtypeStruct((3 * CH, D), F32),
@@ -1172,8 +1178,8 @@
             *mlp,
             *[jax.ShapeDtypeStruct((1, CH), F32)] * 4,
         ),
-        in_specs=[VMEM] * 5,
-        out_specs=(VMEM,) * 13,
+        in_specs=[VMEM] * 7,
+        out_specs=(VMEM,) * 15,
         compiler_params=pltpu.CompilerParams(vmem_limit_bytes=LIMIT),
         name="final",
     )(*operands)
@@ -1190,16 +1196,18 @@
     x = inputs.T
     (
         scaling, features, x1, x2, na, qkv, wa, wat, gains_all,
-        lse, of, go_heads, gx3, out, n3_all, gwo, gmlp_b, ggain_b,
+        lse, of, go_heads, gx3, out, n3, gwo, gmlp_b, ggain_b,
     ) = first(
         shape_pick, x, out_grad.T, gains, filters, weight,
         gate_a, up_a, down_a, qkv_weight.T, out_weight, gate_b, up_b, down_b,
     )
     gx, joint, gat, ga, gb, gain_sum = second(
         shape_pick, x, scaling, features, x1, x2, na, qkv, wa, wat, gains_all,
-        lse, of, go_heads, gx3, n3_all, gwo, gmlp_b, ggain_b, gains, filters, weight,
+        lse, of, go_heads, gx3, n3, gwo, gmlp_b, ggain_b, gains, filters, weight,
     )
-    gws, gate_ga, up_ga, down_ga, gqkv, gout, gate_gb, up_gb, down_gb, *gain_grads = final(joint, gat, ga, gb, gain_sum)
+    out, gx, gws, gate_ga, up_ga, down_ga, gqkv, gout, gate_gb, up_gb, down_gb, *gain_grads = final(
+        joint, gat, ga, gb, gain_sum, out, gx
+    )
     gain_a, gain_n, gain_b, gain_s = (grad.reshape(CH) for grad in gain_grads)
     return (
         out.T, gx.T, gain_s, gws.reshape(K + LAGS, CH, D), gain_a, gate_ga, up_ga, down_ga,

time: 210 us -> 201 us (0.957)
  Pallas kernels: 205 us -> 197 us
    pallas_call x1, Pallas kernels: 101 us -> 92.9 us  [first(): pl.pallas_call(first_kernel, out_shape=(jax.ShapeDtypeStruct((1, T), F32)...]
where the time goes in v2:
time: 201 us; the launch traced here: 200 us
  Pallas kernels  197 us (98%)
    pallas_call x1, Pallas kernels, second(): pl.pallas_call(second_kernel, out_shape=(jax.ShapeDtypeStruct((CH, T), F3...  100 us
    pallas_call x1, Pallas kernels, first(): pl.pallas_call(first_kernel, out_shape=(jax.ShapeDtypeStruct((1, T), F32)...  92.9 us

profile of v2, /device:TPU:0, one launch (start us, length us, event | category | flops | bytes accessed | tf_op | source)
XLA Modules:
  0.0 199.8 jit_solution(14490413433012705346)
XLA Ops:
  1.3 0.7 pad_maximum_fusion
  2.0 0.1 copy.36
  2.1 0.6 pad.4.gains_ref
  2.7 92.9 %first.1 = (f32[1,2048]{1,0:T(1,128)}, bf16[864,2048]{1,0:T(8,128)(2,1)}, f32[512,128]{1,0:T(8,128)}, f32[512,128]{1,0:T(8,128)}, bf16[512,256]{1,0:T(8,128)(2,1...) custom-call(s32[1]{0:T(128)S(6)} %copy.37.pick_ref, ...), custom_call_target="tpu_custom_call" | custom-call | tf_op jit(solution)/shard_map/first/pallas_call | solution.py:692
  95.7 100.4 %second.1 = (f32[32,2048]{1,0:T(8,128)}, bf16[896,512]{1,0:T(8,128)(2,1)}, bf16[128,512]{1,0:T(8,128)(2,1)}, bf16[384,512]{1,0:T(8,128)(2,1)}, bf16[384,512]{1,0:T(8,128)(2,1)}, /*index=5*/f32[8,128]{1,0:T(8,128)}) custom-call(s32[1]{0:T(128)S(6)} %copy.37.pick_ref, bf16[32,2048]{1,0:T(8,128)(2,1)} %bitcast.19, f32[1,2048]{1,0:T(1,128)} %get-tuple-element.54.scale_ref, ...), custom_call_target="tpu_custom_call" | custom-call | tf_op jit(solution)/shard_map/second/pallas_call | solution.py:1083
  196.0 3.7 %final.1 = (bf16[32,2048]{1,0:T(8,128)(2,1)}, f32[32,2048]{1,0:T(8,128)}, f32[864,512]{1,0:T(8,128)}, f32[512,128]{1,0:T(8,128)}, f32[512,128]{1,0:T(8,128)}, /*...) custom-call(bf16[896,512]{1,0:T(8,128)(2,1)} %get-tuple-element.71.j, ...), custom_call_target="tpu_custom_call" | custom-call | tf_op jit(solution)/shard_map/final/pallas_call | solution.py:1169

commit v3 on v2

--- a/solution.py
+++ b/solution.py
@@ -169,7 +169,9 @@
         beside = buf.at[:, half(place.beside)]
         self.to_beside = remote(own, own, sem, 0, place.beside)
         self.to_z = [remote(own, own, sem, step, place.along_z(step)) for step in self.steps]
-        self.relays = [remote(beside, beside, sem, 3 + step, place.along_z(step)) for step in self.steps]
+        farthest = buf.at[:, half(((place.z + 2) % 4) * 4 + me % 4)]
+        self.relays = [remote(beside, beside, sem, 3 + step, place.along_z(step)) for step in self.steps[:2]]
+        self.relays.append(remote(farthest, farthest, sem, 5, place.beside))
         self.forwards = [remote(own, own, sem, 7, place.partner), remote(beside, beside, sem, 8, place.partner)]
         for step in self.steps:
             for shift, other in ((8, me), (11, place.beside)):
@@ -183,12 +185,18 @@
 
     def relay(self):
         self.to_beside.wait_recv()
-        for copy in [*self.relays, self.forwards[1]]:
+        for copy in [*self.relays[:2], self.forwards[1]]:
             copy.start()
 
+    def cross(self):
+        self.to_z[2].wait_recv()
+        self.relays[2].start()
+        self.forwards[6].start()
+
     def arrive(self, index):
-        self.to_z[index].wait_recv()
-        self.forwards[2 + 2 * index].start()
+        if index < 2:
+            self.to_z[index].wait_recv()
+            self.forwards[2 + 2 * index].start()
         self.relays[index].wait_recv()
         self.forwards[3 + 2 * index].start()
 
@@ -255,8 +263,9 @@
 
 
 class GradientSum:
-    def __init__(self, place, parts, done, bufs, sem, begin, each, y_first):
+    def __init__(self, place, parts, done, bufs, sem, begin, each, y_first, source=None):
         self.place, self.parts, self.done, self.sem = place, parts, done, sem
+        self.source = parts if source is None else source
         self.got, self.sum_1, self.got_2, self.sum_2, self.z_got = bufs
         self.begin, self.each, self.y_first = begin, each, y_first
         self.copies = []
@@ -278,7 +287,7 @@
     def first(self):
         count = self.each * (4 if self.y_first else 2)
         for slot, (there, target) in enumerate(self.to_y if self.y_first else self.to_x):
-            self.send(self.parts.at[:, self.at(there, count, self.begin)], self.got.at[slot], target)
+            self.send(self.source.at[:, self.at(there, count, self.begin)], self.got.at[slot], target)
 
     def second(self):
         place, each = self.place, self.each
@@ -311,14 +320,21 @@
         index = place.ylo * 4 + place.x if self.y_first else place.x * 2 + place.ylo
         mine = self.at(index, each, self.begin)
         self.done[mine, :] = value.astype(BF16)
-        for step in range(1, DP):
-            self.send(self.done.at[mine], self.done.at[mine], {"dp": place.along_dp(step)})
+        for _, target in self.to_x:
+            self.send(self.done.at[mine], self.done.at[mine], target)
+
+    def back_y(self):
+        place, each = self.place, self.each
+        self.arrived(3)
+        for x in range(4):
+            index = place.ylo * 4 + x if self.y_first else x * 2 + place.ylo
+            part = self.done.at[self.at(index, each, self.begin)]
+            self.send(part, part, self.to_y[0][1])
 
     def close(self):
-        for copy in self.copies[:7]:
+        self.arrived(4)
+        for copy in self.copies:
             copy.wait_send()
-        for copy in self.copies[7:]:
-            copy.wait()
 
 
 def sum_buffers(each, y_first):
@@ -334,9 +350,9 @@
 
 
 def first_kernel(
-    pick_ref, x_ref, go_ref, gains_ref, taps_ref, weight_ref,
+    pick_ref, x_ref, go_ref, gain_a, gain_n, gain_b_in, gain_s, taps_ref, weight_ref,
     gate_a, up_a, down_a, qkv_w, out_w, gate_b, up_b, down_b,
-    scale_ref, feat_out, x1_ref, x2_ref, na_out, qkv_out, wa_out, wat_out, gains_all,
+    gains_ref, scale_ref, feat_out, x1_ref, x2_ref, na_out, qkv_out, wa_out, wat_out, gains_all,
     lse_ref, of_ref, go_heads, gx3_ref, out_ref, n3_ref, gwo_ref, gmlp_ref, ggain_ref,
     feat_ref, na_ref, qkv_ref, wa_ref, wat_ref, streams, streams_own, go2, squares, taps, table, table_late, weight_t, blocks, y_ref,
     core_got, chip_got, parts, got, heads, wb_ref, keys, values, own_heads, all_heads, x3_ref, nb, nb_got, go_got,
@@ -359,6 +375,10 @@
         ref[0, 0, :OWN] = gate[...].T
         ref[0, 0, OWN : 2 * OWN] = up[...].T
         ref[0, 0, 2 * OWN :] = down[...]
+    lines = [ref[...].astype(F32) for ref in (gain_a, gain_n, gain_b_in, gain_s)]
+    lines = jnp.concatenate(lines + [jnp.zeros((OWN - 4, CH), F32)], axis=0)
+    lines = jnp.concatenate([lines, jnp.zeros((OWN, OWN - CH), F32)], axis=1)
+    gains_ref[...] = lines.T[:CH].astype(BF16)
     streams[0] = x_ref[...]
     streams[1] = go_ref[...]
     for index in range(MP):
@@ -572,6 +592,15 @@
     move_n.wait_send()
     move_z.wait_send()
     spread(qkv_ref, keys, values)
+    targets = [place.quarters[slot // 4] * 4 + slot % 4 for slot in range(8)]
+    copies = [
+        pltpu.make_async_remote_copy(
+            src_ref=own_heads.at[slot], dst_ref=all_heads.at[chip],
+            send_sem=sem_o.at[0, slot], recv_sem=sem_o.at[1, chip],
+            device_id={"mp": targets[slot]}, device_id_type=MESH,
+        )
+        for slot in range(8)
+    ]
     for part in range(2):
         quarter = place.quarters[part]
         queries = query_block(qkv_ref, quarter)
@@ -592,22 +621,12 @@
         of_ref[part] = total
         for index in range(4):
             own_heads[part * 4 + index] = total[:, index * OWN : (index + 1) * OWN].astype(BF16)
-    targets = [place.quarters[slot // 4] * 4 + slot % 4 for slot in range(8)]
-    copies = [
-        pltpu.make_async_remote_copy(
-            src_ref=own_heads.at[slot], dst_ref=all_heads.at[chip],
-            send_sem=sem_o.at[0, slot], recv_sem=sem_o.at[1, chip],
-            device_id={"mp": targets[slot]}, device_id_type=MESH,
-        )
-        for slot in range(8)
-    ]
-    for slot in range(8):
-        pl.when(targets[slot] != me)(copies[slot].start)
-
-        @pl.when(targets[slot] == me)
-        def _():
-            all_heads[chip] = own_heads[slot]
-
+        for slot in range(part * 4, part * 4 + 4):
+            pl.when(targets[slot] != me)(copies[slot].start)
+
+            @pl.when(targets[slot] == me)
+            def _():
+                all_heads[chip] = own_heads[slot]
     arrivals = [
         remote(own_heads.at[0], all_heads.at[head], sem_o, head, place.partner) for head in range(CHIPS)
     ]
@@ -692,6 +711,7 @@
     return pl.pallas_call(
         first_kernel,
         out_shape=(
+            jax.ShapeDtypeStruct((CH, OWN), BF16),
             jax.ShapeDtypeStruct((1, T), F32),
             jax.ShapeDtypeStruct((FEAT, T), BF16),
             jax.ShapeDtypeStruct((D, OWN), F32),
@@ -711,8 +731,8 @@
             jax.ShapeDtypeStruct((4, 3 * OWN, D), BF16),
             jax.ShapeDtypeStruct((D, 1), F32),
         ),
-        in_specs=[SMEM] + [VMEM] * 13,
-        out_specs=(VMEM, ANY, VMEM, VMEM, ANY, ANY, ANY, ANY) + (VMEM,) * 10,
+        in_specs=[SMEM] + [VMEM] * 16,
+        out_specs=(VMEM, VMEM, ANY, VMEM, VMEM, ANY, ANY, ANY, ANY) + (VMEM,) * 10,
         scratch_shapes=[
             pltpu.VMEM((FEAT, T), BF16),
             pltpu.VMEM((D, 2 * OWN), BF16),
@@ -765,9 +785,9 @@
 
 def second_kernel(
     pick_ref, x_ref, scale_ref, feat_in, x1_ref, x2_ref, na_ref, qkv_ref, wa_in, wat_in, gains_all,
-    lse_ref, of_ref, go_heads, gx3_ref, n3_ref, gwo_ref, gmlp_b, ggain_b, gains_ref, taps_ref, weight_in,
+    lse_ref, of_ref, go_heads, gx3_ref, n3_ref, gwo_in, gmlp_in, ggain_b, gains_ref, taps_ref, weight_in,
     gx_ref, joint_ref, sum_t, sum_a, sum_b, gain_sum,
-    feat_ref, wa_ref, wat_ref, n3_all, weight_ref,
+    feat_ref, wa_ref, wat_ref, n3_all, weight_ref, gmlp_b, gwo_own,
     keys, values, kv_grad, q_grad, mine, core_got, chip_sum, head_grads, gz, gz_got, na_got, parts, got,
     acts, acts_got, gy1_ref, row_got, q_rows, gwo_got,
     b_1, b_2, b_3, b_4, b_5, gmlp_a, a_1, a_2, a_3, a_4, a_5, a_6, a_7, a_8, a_9, a_10, gat, gat_got, ggain_ref, gain_own, gain_dp,
@@ -781,7 +801,8 @@
     n3_all[:, half(me)] = n3_ref[...]
     loads = []
     for src, dst in (
-        (wat_in, wat_ref), (wa_in, wa_ref), (feat_in, feat_ref), (weight_in, weight_ref)
+        (wat_in, wat_ref), (wa_in, wa_ref), (feat_in, feat_ref), (weight_in, weight_ref),
+        (gmlp_in, gmlp_b), (gwo_in.at[me], gwo_own),
     ):
         copy = pltpu.make_async_copy(src, dst, sem_load.at[len(loads)])
         copy.start()
@@ -792,7 +813,7 @@
     )
     gain_a = gains_all[:, 0:1].astype(F32)
     gain_n = gains_all[:, 1:2].astype(F32)
-    sum_of_b = GradientSum(place, gmlp_b, sum_b, (b_1, b_2, b_3, b_4, b_5), sem_b, 0, 48, False)
+    sum_of_b = GradientSum(place, gmlp_b, sum_b, (b_1, b_2, b_3, b_4, b_5), sem_b, 0, 48, False, gmlp_in)
     sums_of_a = (
         GradientSum(place, gmlp_a, sum_a, (a_1, a_2, a_3, a_4, a_5), sem_a, 0, 32, False),
         GradientSum(place, gmlp_a, sum_a, (a_6, a_7, a_8, a_9, a_10), sem_a2, 256, 16, True),
@@ -829,7 +850,7 @@
             o_first = []
             for step in range(1, MP):
                 there = place.around(step)
-                copy = remote(gwo_ref.at[there], gwo_got.at[step - 1], sem_gwo, step - 1, there)
+                copy = remote(gwo_in.at[there], gwo_got.at[step - 1], sem_gwo, step - 1, there)
                 copy.start()
                 o_first.append(copy)
     for index in range(MP):
@@ -870,6 +891,7 @@
     gx2 = gx3_ref[...] + stream_grad
     gz[:, :OWN] = gx2.astype(BF16)
     move_gz = swap(place, gz.at[:, :OWN], gz.at[:, OWN:], sem_n)
+    loads[4].wait()
     sum_of_b.second()
     loads[1].wait()
     weights = hidden_weights(wa_ref)
@@ -886,6 +908,7 @@
     ]
     sum_of_b.third()
     gather_n3.relay()
+    gather_n3.cross()
     for copy in shares:
         copy.wait_recv()
     hidden_weight_grads(acts, acts_got, ((na_ref, na_got), (na_ref, na_got), (gz, gz_got)), gmlp_a)
@@ -910,7 +933,8 @@
     gat[: 3 * CH] = nt(q_rows[...], n3_all[...]).astype(BF16)
     for copy in o_first:
         copy.wait_recv()
-    value = gwo_ref[me].astype(F32)
+    loads[5].wait()
+    value = gwo_own[...].astype(F32)
     for index in range(MP - 1):
         value = value + gwo_got[index].astype(F32)
     gat[3 * CH :] = value.astype(BF16)
@@ -920,6 +944,7 @@
         copy = remote(gat.at[rows(there, 16)], gat_got.at[step - 1], sem_t, step - 1, {"dp": there})
         copy.start()
         t_first.append(copy)
+    sum_of_b.back_y()
     gather_gy1.relay()
     reverse_taps(taps_ref, reverse)
 
@@ -946,6 +971,7 @@
     loads[3].wait()
     build_some(0, 4)
     gather_gy1.joined(-1)
+    gather_gy1.cross()
     absorb(place.z)
     gather_gy1.arrive(0)
     build_some(4, 8)
@@ -1064,6 +1090,8 @@
     value = jnp.concatenate([value[index : index + 1] for index in range(4)], axis=1)
     stream_grad = scaled * scaling - stream * (scaling * scaling * scaling * value / D)
     gx_ref[...] = stream_grad + gy1_ref[rows(me, CH), :].astype(F32)
+    for part in sums_of_a:
+        part.back_y()
     for copy in last:
         copy.wait()
     value = gain_own[...]
@@ -1074,9 +1102,8 @@
         copy.wait_send()
     gather_n3.close()
     gather_gy1.close()
-    for part in sums_of_a:
+    for part in (sum_of_b, *sums_of_a):
         part.close()
-    sum_of_b.close()
 
 
 def second(*operands):
@@ -1090,7 +1117,11 @@
             jax.ShapeDtypeStruct((3 * OWN, D), BF16),
             jax.ShapeDtypeStruct((8, OWN), F32),
         ),
-        in_specs=[SMEM, VMEM, VMEM, ANY, VMEM, VMEM, VMEM, VMEM, ANY, ANY] + [VMEM] * 11 + [ANY],
+        in_specs=[SMEM, VMEM, VMEM, ANY, VMEM, VMEM, VMEM, VMEM, ANY, ANY]
+        + [VMEM] * 6
+        + [ANY, ANY]
+        + [VMEM] * 3
+        + [ANY],
         out_specs=(VMEM,) * 6,
         scratch_shapes=[
             pltpu.VMEM((FEAT, T), BF16),
@@ -1098,6 +1129,8 @@
             pltpu.VMEM((CHIPS, 2, OWN, D), BF16),
             pltpu.VMEM((D, T), BF16),
             pltpu.VMEM((FEAT, D), BF16),
+            pltpu.VMEM((4, 3 * OWN, D), BF16),
+            pltpu.VMEM((CH, D), BF16),
             pltpu.VMEM((HD, T), BF16),
             pltpu.VMEM((HD, T), BF16),
             pltpu.VMEM((T, 2 * HD), F32),
@@ -1138,7 +1171,7 @@
             pltpu.VMEM((MP, 8, D), F32),
             sems(15), sems(1), sems(1), sems(15), sems(15), sems(1), sems(14), sems(14), sems(14), sems(7), sems(7),
             sems(7), sems(7), sems(7), sems(15), sems(3), sems(15),
-            pltpu.SemaphoreType.DMA((4,)),
+            pltpu.SemaphoreType.DMA((6,)),
         ],
         compiler_params=pltpu.CompilerParams(
             collective_id=1, has_side_effects=True, vmem_limit_bytes=LIMIT
@@ -1190,20 +1223,19 @@
     mlp_gain_a, gate_a, up_a, down_a, attn_gain, qkv_weight, out_weight,
     mlp_gain_b, gate_b, up_b, down_b,
 ):
-    gains = jnp.stack([mlp_gain_a, attn_gain, mlp_gain_b, stu_gain], axis=1)
-    gains = jnp.pad(gains, ((0, 0), (0, OWN - 4)))
+    gains = [gain.reshape(1, CH) for gain in (mlp_gain_a, attn_gain, mlp_gain_b, stu_gain)]
     weight = stu_weight.reshape(FEAT, D)
     x = inputs.T
     (
-        scaling, features, x1, x2, na, qkv, wa, wat, gains_all,
+        gains_own, scaling, features, x1, x2, na, qkv, wa, wat, gains_all,
         lse, of, go_heads, gx3, out, n3, gwo, gmlp_b, ggain_b,
     ) = first(
-        shape_pick, x, out_grad.T, gains, filters, weight,
+        shape_pick, x, out_grad.T, *gains, filters, weight,
         gate_a, up_a, down_a, qkv_weight.T, out_weight, gate_b, up_b, down_b,
     )
     gx, joint, gat, ga, gb, gain_sum = second(
         shape_pick, x, scaling, features, x1, x2, na, qkv, wa, wat, gains_all,
-        lse, of, go_heads, gx3, n3, gwo, gmlp_b, ggain_b, gains, filters, weight,
+        lse, of, go_heads, gx3, n3, gwo, gmlp_b, ggain_b, gains_own, filters, weight,
     )
     out, gx, gws, gate_ga, up_ga, down_ga, gqkv, gout, gate_gb, up_gb, down_gb, *gain_grads = final(
         joint, gat, ga, gb, gain_sum, out, gx

time: 201 us -> 199 us (0.990)
  no operation moved by 1% of the time
where the time goes in v3:
time: 199 us
  Pallas kernels  197 us (99%)
    pallas_call x1, Pallas kernels, second(): pl.pallas_call(second_kernel, out_shape=(jax.ShapeDtypeStruct((CH, T), F3...  101 us
    pallas_call x1, Pallas kernels, first(): pl.pallas_call(first_kernel, out_shape=(jax.ShapeDtypeStruct((CH, OWN), B...  92.7 us

profile of v3, /device:TPU:0, one launch (start us, length us, event | category | flops | bytes accessed | tf_op | source)
XLA Modules:
  0.0 198.5 jit_solution(11484529511498814194)
XLA Ops:
  1.3 92.7 %first.1 = (bf16[32,128]{1,0:T(8,128)(2,1)}, f32[1,2048]{1,0:T(1,128)}, bf16[864,2048]{1,0:T(8,128)(2,1)}, f32[512,128]{1,0:T(8,128)}, f32[512,128]{1,0:T(8,128)...) custom-call(s32[1]{0:T(128)S(6)} %copy.32.pick_ref, ...), custom_call_target="tpu_custom_call" | custom-call | tf_op jit(solution)/shard_map/first/pallas_call | solution.py:711
  94.0 100.7 %second.1 = (f32[32,2048]{1,0:T(8,128)}, bf16[896,512]{1,0:T(8,128)(2,1)}, bf16[128,512]{1,0:T(8,128)(2,1)}, bf16[384,512]{1,0:T(8,128)(2,1)}, bf16[384,512]{1,0:T(8,128)(2,1)}, /*index=5*/f32[8,128]{1,0:T(8,128)}) custom-call(s32[1]{0:T(128)S(6)} %copy.32.pick_ref, bf16[32,2048]{1,0:T(8,128)(2,1)} %bitcast.19, f32[1,2048]{1,0:T(1,128)} %get-tuple-element.55.scale_ref, ...), custom_call_target="tpu_custom_call" | custom-call | tf_op jit(solution)/shard_map/second/pallas_call | solution.py:1110
  194.7 3.7 %final.1 = (bf16[32,2048]{1,0:T(8,128)(2,1)}, f32[32,2048]{1,0:T(8,128)}, f32[864,512]{1,0:T(8,128)}, f32[512,128]{1,0:T(8,128)}, f32[512,128]{1,0:T(8,128)}, /*...) custom-call(bf16[896,512]{1,0:T(8,128)(2,1)} %get-tuple-element.73.j, ...), custom_call_target="tpu_custom_call" | custom-call | tf_op jit(solution)/shard_map/final/pallas_call | solution.py:1202

commit v4 on v3

--- a/solution.py
+++ b/solution.py
@@ -944,7 +944,6 @@
         copy = remote(gat.at[rows(there, 16)], gat_got.at[step - 1], sem_t, step - 1, {"dp": there})
         copy.start()
         t_first.append(copy)
-    sum_of_b.back_y()
     gather_gy1.relay()
     reverse_taps(taps_ref, reverse)
 
@@ -974,6 +973,7 @@
     gather_gy1.cross()
     absorb(place.z)
     gather_gy1.arrive(0)
+    sum_of_b.back_y()
     build_some(4, 8)
     gather_gy1.joined(0)
     absorb((place.z + 3) % 4)

time: 199 us -> 197 us (0.990)
  no operation moved by 1% of the time
where the time goes in v4:
time: 197 us
  Pallas kernels  196 us (99%)
    pallas_call x1, Pallas kernels, second(): pl.pallas_call(second_kernel, out_shape=(jax.ShapeDtypeStruct((CH, T), F3...  99.2 us
    pallas_call x1, Pallas kernels, first(): pl.pallas_call(first_kernel, out_shape=(jax.ShapeDtypeStruct((CH, OWN), B...  92.7 us

profile of v4, /device:TPU:0, one launch (start us, length us, event | category | flops | bytes accessed | tf_op | source)
XLA Modules:
  0.0 197.0 jit_solution(7433241029634053683)
XLA Ops:
  1.3 92.7 %first.1 = (bf16[32,128]{1,0:T(8,128)(2,1)}, f32[1,2048]{1,0:T(1,128)}, bf16[864,2048]{1,0:T(8,128)(2,1)}, f32[512,128]{1,0:T(8,128)}, f32[512,128]{1,0:T(8,128)...) custom-call(s32[1]{0:T(128)S(6)} %copy.32.pick_ref, ...), custom_call_target="tpu_custom_call" | custom-call | tf_op jit(solution)/shard_map/first/pallas_call | solution.py:711
  94.0 99.2 %second.1 = (f32[32,2048]{1,0:T(8,128)}, bf16[896,512]{1,0:T(8,128)(2,1)}, bf16[128,512]{1,0:T(8,128)(2,1)}, bf16[384,512]{1,0:T(8,128)(2,1)}, bf16[384,512]{1,0:T(8,128)(2,1)}, /*index=5*/f32[8,128]{1,0:T(8,128)}) custom-call(s32[1]{0:T(128)S(6)} %copy.32.pick_ref, bf16[32,2048]{1,0:T(8,128)(2,1)} %bitcast.19, f32[1,2048]{1,0:T(1,128)} %get-tuple-element.55.scale_ref, ...), custom_call_target="tpu_custom_call" | custom-call | tf_op jit(solution)/shard_map/second/pallas_call | solution.py:1110
  193.2 3.7 %final.1 = (bf16[32,2048]{1,0:T(8,128)(2,1)}, f32[32,2048]{1,0:T(8,128)}, f32[864,512]{1,0:T(8,128)}, f32[512,128]{1,0:T(8,128)}, f32[512,128]{1,0:T(8,128)}, /*...) custom-call(bf16[896,512]{1,0:T(8,128)(2,1)} %get-tuple-element.73.j, ...), custom_call_target="tpu_custom_call" | custom-call | tf_op jit(solution)/shard_map/final/pallas_call | solution.py:1202

commit v5 on v4

--- a/solution.py
+++ b/solution.py
@@ -820,6 +820,17 @@
     )
     pick = pick_ref[0]
     spread(qkv_ref, keys, values)
+    arrived()
+    gather_n3 = Gather(place, n3_all, sem_all)
+    gather_n3.begin()
+    share_n = share(place, na_ref, na_got, sem_act, 0)
+    sum_of_b.first()
+    o_first = []
+    for step in range(1, MP):
+        there = place.around(step)
+        copy = remote(gwo_in.at[there], gwo_got.at[step - 1], sem_gwo, step - 1, there)
+        copy.start()
+        o_first.append(copy)
     for part in range(2):
         quarter = place.quarters[part]
         queries = query_block(qkv_ref, quarter)
@@ -841,18 +852,6 @@
                 both = both + kv_grad[here]
             kv_grad[here] = both
         q_grad[part] = (query_grad * HD**-0.5).astype(BF16)
-        if part == 0:
-            arrived()
-            gather_n3 = Gather(place, n3_all, sem_all)
-            gather_n3.begin()
-            share_n = share(place, na_ref, na_got, sem_act, 0)
-            sum_of_b.first()
-            o_first = []
-            for step in range(1, MP):
-                there = place.around(step)
-                copy = remote(gwo_in.at[there], gwo_got.at[step - 1], sem_gwo, step - 1, there)
-                copy.start()
-                o_first.append(copy)
     for index in range(MP):
         mine[index // 2, index % 2, :HD] = jnp.zeros((HD, OWN), BF16)
         mine[index // 2, index % 2, HD:] = kv_grad[index * OWN : (index + 1) * OWN].T.astype(BF16)

time: 197 us -> 197 us (level)
  no operation moved by 1% of the time
where the time goes in v5:
time: 197 us
  Pallas kernels  196 us (99%)
    pallas_call x1, Pallas kernels, second(): pl.pallas_call(second_kernel, out_shape=(jax.ShapeDtypeStruct((CH, T), F3...  99.3 us
    pallas_call x1, Pallas kernels, first(): pl.pallas_call(first_kernel, out_shape=(jax.ShapeDtypeStruct((CH, OWN), B...  92.7 us

profile of v5, /device:TPU:0, one launch (start us, length us, event | category | flops | bytes accessed | tf_op | source)
XLA Modules:
  0.0 197.1 jit_solution(1365084089142402113)
XLA Ops:
  1.3 92.7 %first.1 = (bf16[32,128]{1,0:T(8,128)(2,1)}, f32[1,2048]{1,0:T(1,128)}, bf16[864,2048]{1,0:T(8,128)(2,1)}, f32[512,128]{1,0:T(8,128)}, f32[512,128]{1,0:T(8,128)...) custom-call(s32[1]{0:T(128)S(6)} %copy.32.pick_ref, ...), custom_call_target="tpu_custom_call" | custom-call | tf_op jit(solution)/shard_map/first/pallas_call | solution.py:711
  94.0 99.3 %second.1 = (f32[32,2048]{1,0:T(8,128)}, bf16[896,512]{1,0:T(8,128)(2,1)}, bf16[128,512]{1,0:T(8,128)(2,1)}, bf16[384,512]{1,0:T(8,128)(2,1)}, bf16[384,512]{1,0:T(8,128)(2,1)}, /*index=5*/f32[8,128]{1,0:T(8,128)}) custom-call(s32[1]{0:T(128)S(6)} %copy.32.pick_ref, bf16[32,2048]{1,0:T(8,128)(2,1)} %bitcast.19, f32[1,2048]{1,0:T(1,128)} %get-tuple-element.55.scale_ref, ...), custom_call_target="tpu_custom_call" | custom-call | tf_op jit(solution)/shard_map/second/pallas_call | solution.py:1109
  193.3 3.7 %final.1 = (bf16[32,2048]{1,0:T(8,128)(2,1)}, f32[32,2048]{1,0:T(8,128)}, f32[864,512]{1,0:T(8,128)}, f32[512,128]{1,0:T(8,128)}, f32[512,128]{1,0:T(8,128)}, /*...) custom-call(bf16[896,512]{1,0:T(8,128)(2,1)} %get-tuple-element.73.j, ...), custom_call_target="tpu_custom_call" | custom-call | tf_op jit(solution)/shard_map/final/pallas_call | solution.py:1201
